TPU v7x, 32 devices: a whole 2x2x4 slice. The times are simulated.
32 devices in a mesh: blk: 8 (over y, x, core), view: 4 (over z).
Axes of the slice: x: 2, y: 2, z: 4, core: 2. Of those that a mesh axis runs over, the one named last changes fastest.
Arguments:
- estimate: float32 [256, 128, 128], P('blk'), may hold values from 0.5 to 1.5
- observed: bfloat16 [4, 256, 128, 128], P('view', 'blk'), may hold values from 0.19921875 to 2
- psf_taps: float32 [4, 2, 3, 31], P('view'), may hold values from 0.05 to 1
- psf_weight: float32 [4, 2], P('view'), may hold values from 0.2 to 1
- shifts: int32 [4, 3], P('view'), may hold values from -8 to 8, as said below
- cover_first: int32 [4], replicated, may hold values from 0 to 6, as said below
- cover_count: int32 [4], replicated, may hold values from 2 to 8, as said below
Outputs:
- joined: float32 [256, 128, 128], P('blk')
Inputs may be any that keep to these rules, and one draw needn't show every extreme that they name: `shifts`: every component of a registration shift lies in -8 .. 8; some view that covers every block has first component 8, and another that covers every block has -8. View v covers the whole blocks cover_first[v] .. cover_first[v] + cover_count[v] - 1, all inside the volume; two or more views cover every block, and some view covers only the last 2 blocks. `cover_count`: together with cover_first, the covered blocks of each view lie within the volume.
All inputs are finite; a program needn't handle non-finite values.
Results may differ from a plain program's by a relative error of at most 0.0003.
Values may be sent and summed in bfloat16 or wider, within the bound.
A program may use at most 128 MiB of HBM per device.

v0:
```python
import jax
import jax.numpy as jnp
from jax import lax
from jax.sharding import PartitionSpec as P

SHIFT_MAX = 8
ROUNDS = 2
HALF_TAPS = 15


OFFSET = 0.1


def padded(block, sides, width):
    for axis, dim in sides:
        count = lax.axis_size(axis)
        forward = [(i, i + 1) for i in range(count - 1)]
        backward = [(target, source) for source, target in forward]
        low = lax.ppermute(
            lax.slice_in_dim(block, block.shape[dim] - width, None, axis=dim), axis, forward
        )
        high = lax.ppermute(lax.slice_in_dim(block, 0, width, axis=dim), axis, backward)
        block = jnp.concatenate([low, block, high], axis=dim)
    return block


def band_matrix(taps, rows, cols, offset):
    diff = (
        lax.broadcasted_iota(jnp.int32, (rows, cols), 1)
        - lax.broadcasted_iota(jnp.int32, (rows, cols), 0)
        + offset
    )
    matrix = jnp.zeros((rows, cols), jnp.float32)
    for place in range(taps.shape[0]):
        matrix = matrix + jnp.where(diff == place, taps[place], jnp.float32(0.0))
    return matrix


def band_set(taps, planes, rows, cols, half):
    result = []
    for rank in range(2):
        result.append(
            (
                band_matrix(taps[rank, 0], planes, planes + 2 * half, 0),
                band_matrix(taps[rank, 1], rows, rows, half),
                band_matrix(taps[rank, 2], cols, cols, half),
            )
        )
    return result


def blur_block(window, mats, weights):
    total = None
    for rank in range(2):
        mat_x, mat_y, mat_z = mats[rank]
        part = jnp.einsum("ij,jyz->iyz", mat_x, window, precision=lax.Precision.HIGHEST)
        part = jnp.einsum("ij,xjz->xiz", mat_y, part, precision=lax.Precision.HIGHEST)
        part = jnp.einsum("ij,xyj->xyi", mat_z, part, precision=lax.Precision.HIGHEST)
        term = weights[rank] * part
        total = term if total is None else total + term
    return total


def estimate_window(field, reach):
    return padded(field.astype(jnp.bfloat16), (("blk", 0),), reach).astype(field.dtype)


def on_device(estimate, observed, psf_taps, psf_weight, shifts, cover_first, cover_count):
    planes, rows, cols = estimate.shape
    half = HALF_TAPS
    view_index = lax.axis_index("view")
    block_index = lax.axis_index("blk")
    taps = psf_taps[0] / jnp.sum(psf_taps[0], axis=-1, keepdims=True)
    weights = psf_weight[0] / jnp.sum(psf_weight[0])
    backward = band_set(taps[:, :, ::-1], planes, rows, cols, half)
    extra = 0
    forward = band_set(taps, planes + 2 * extra, rows, cols, half)
    slots = lax.broadcasted_iota(jnp.int32, cover_first.shape, 0)
    inside = (block_index >= cover_first) & (block_index < cover_first + cover_count)
    covered = jnp.sum(jnp.where(inside, 1.0, 0.0))
    owned = jnp.sum(jnp.where(inside & (slots == view_index), 1.0, 0.0))
    weight_view = owned / covered
    extended = padded(observed[0], (("blk", 0),), SHIFT_MAX + extra)
    extended = jnp.pad(extended, ((0, 0), (SHIFT_MAX, SHIFT_MAX), (SHIFT_MAX, SHIFT_MAX)))
    start = (SHIFT_MAX + shifts[0, 0], SHIFT_MAX + shifts[0, 1], SHIFT_MAX + shifts[0, 2])
    registered = lax.dynamic_slice(extended, start, (planes + 2 * extra, rows, cols)).astype(
        jnp.float32
    )
    field = estimate
    for step in range(ROUNDS):
        window = estimate_window(field, half + extra)
        blurred = blur_block(window, forward, weights)
        ratio = (registered + OFFSET) / (blurred + OFFSET)
        ratio_window = padded(ratio.astype(jnp.bfloat16), (("blk", 0),), half).astype(ratio.dtype)
        correction = blur_block(ratio_window, backward, weights)
        weighted_log = weight_view * jnp.log(correction)
        field = field * jnp.exp(lax.psum(weighted_log, "view"))
    return field


def solution(mesh):
    placed = (
        P("blk", None, None),
        P("view", "blk", None, None),
        P("view", None, None, None),
        P("view", None),
        P("view", None),
        P(),
        P(),
    )
    return jax.shard_map(
        on_device, mesh=mesh, in_specs=placed, out_specs=P("blk", None, None), check_vma=False
    )
```

profile of v0, /device:TPU:0, one launch (start us, length us, event | category | flops | bytes accessed | tf_op | source)
XLA Modules:
  0.0 812.8 jit_solution(9598499088466406485)
XLA Ops:
  48.3 21.3 %fusion.54 = f32[32,128,128]{2,0,1:T(8,128)S(1)} fusion(bf16[62,128,128]{2,1,0:T(8,128)(2,1)S(1)} %pad_maximum_fusion, f32[]{:T(128)} %bitcast.140, f32[]{:T(128)} %bitcast.139, f32[]{:T(128)} %bitcast.138, f32[]{:T(128)} %bitcast.137, f32[]{:T(128)} %bitcast.136, f32[]{:T(128)} %bitcast.135, f32[]{:T(128)} %bitcast.134, f32[]{:T(128)} %bitcast.133, ...), kind=kOutput, calls=%fused_computation.73 | convolution fusion | flops 390254784 | bytes 4128892 | tf_op jit(solution)/shard_map/ij,jyz->iyz/dot_general | solution.py:56
  69.6 21.8 %fusion.56 = f32[32,128,128]{2,0,1:T(8,128)S(1)} fusion(bf16[62,128,128]{2,1,0:T(8,128)(2,1)S(1)} %pad_maximum_fusion, f32[]{:T(128)} %bitcast.32, f32[]{:T(128)} %bitcast.31, f32[]{:T(128)} %bitcast.30, f32[]{:T(128)} %bitcast.29, f32[]{:T(128)} %bitcast.28, f32[]{:T(128)} %bitcast.27, f32[]{:T(128)} %bitcast.26, f32[]{:T(128)} %bitcast.25, f32[]{:T(128)} %bitcast.24, ...), kind=kOutput, calls=%fused_computation.75 | convolution fusion | flops 390254784 | bytes 4128892 | tf_op jit(solution)/shard_map/ij,jyz->iyz/dot_general | solution.py:56
  91.4 22.7 %fusion.36 = f32[32,128,128]{1,2,0:T(8,128)S(1)} fusion(f32[32,128,128]{2,0,1:T(8,128)S(1)} %fusion.54, f32[]{:T(128)} %bitcast.172, f32[]{:T(128)} %bitcast.171, f32[]{:T(128)} %bitcast.170, f32[]{:T(128)} %bitcast.169, f32[]{:T(128)} %bitcast.168, f32[]{:T(128)} %bitcast.167, f32[]{:T(128)} %bitcast.166, f32[]{:T(128)} %bitcast.165, f32[]{:T(128)} %bitcast.164, ...), kind=kOutput, calls=%fused_computation.43 | convolution fusion | flops 806846464 | bytes 4194428 | tf_op jit(solution)/shard_map/ij,xjz->xiz/dot_general | solution.py:57
  114.1 21.5 %fusion.20 = f32[32,128,128]{2,1,0:T(8,128)S(1)} fusion(f32[32,128,128]{1,2,0:T(8,128)S(1)} %fusion.36, f32[]{:T(128)} %bitcast.205, f32[]{:T(128)} %bitcast.204, f32[]{:T(128)} %bitcast.203, f32[]{:T(128)} %bitcast.202, f32[]{:T(128)} %bitcast.201, f32[]{:T(128)} %bitcast.200, f32[]{:T(128)} %bitcast.199, f32[]{:T(128)} %bitcast.198, f32[]{:T(128)} %bitcast.197, ...), kind=kOutput, calls=%fused_computation.27 | convolution fusion | flops 806846464 | bytes 4194428 | tf_op jit(solution)/shard_map/ij,xyj->xyi/dot_general | solution.py:58
  135.7 22.3 %fusion.38 = f32[32,128,128]{1,2,0:T(8,128)S(1)} fusion(f32[32,128,128]{2,0,1:T(8,128)S(1)} %fusion.56, f32[]{:T(128)} %bitcast.74, f32[]{:T(128)} %bitcast.73, f32[]{:T(128)} %bitcast.72, f32[]{:T(128)} %bitcast.71, f32[]{:T(128)} %bitcast.70, f32[]{:T(128)} %bitcast.69, f32[]{:T(128)} %bitcast.68, f32[]{:T(128)} %bitcast.67, f32[]{:T(128)} %bitcast.66, ...), kind=kOutput, calls=%fused_computation.45 | convolution fusion | flops 806846464 | bytes 4194428 | tf_op jit(solution)/shard_map/ij,xjz->xiz/dot_general | solution.py:57
  158.0 23.0 %divide_convert_fusion.1 = bf16[32,128,128]{2,1,0:T(8,128)(2,1)S(1)} fusion(f32[32,128,128]{2,1,0:T(8,128)S(1)} %fusion.20, bf16[32,128,128]{2,1,0:T(8,128)(2,1)S(1)} %fusion.66, f32[32,128,128]{1,2,0:T(8,128)S(1)} %fusion.38, f32[]{:T(128)} %bitcast.109, f32[]{:T(128)} %bitcast, f32[]{:T(128)} %bitcast.107, f32[]{:T(128)} %bitcast.106, f32[]{:T(128)} %bitcast.105, ...), kind=kOutput, calls=%fused_computation.52 | convolution fusion | flops 811040768 | bytes 6291588 | tf_op jit(solution)/shard_map/ij,xyj->xyi/dot_general | solution.py:58
  210.2 21.3 %fusion.52 = f32[32,128,128]{2,0,1:T(8,128)S(1)} fusion(bf16[62,128,128]{2,1,0:T(8,128)(2,1)S(1)} %pad_maximum_fusion.1, f32[]{:T(128)} %bitcast.32, f32[]{:T(128)} %bitcast.31, f32[]{:T(128)} %bitcast.30, f32[]{:T(128)} %bitcast.29, f32[]{:T(128)} %bitcast.28, f32[]{:T(128)} %bitcast.27, f32[]{:T(128)} %bitcast.26, f32[]{:T(128)} %bitcast.25, ...), kind=kOutput, calls=%fused_computation.71 | convolution fusion | flops 390254784 | bytes 4128892 | tf_op jit(solution)/shard_map/ij,jyz->iyz/dot_general | solution.py:56
  231.5 22.7 %fusion.32 = f32[32,128,128]{1,2,0:T(8,128)S(1)} fusion(f32[32,128,128]{2,0,1:T(8,128)S(1)} %fusion.50, f32[]{:T(128)} %bitcast.172, f32[]{:T(128)} %bitcast.171, f32[]{:T(128)} %bitcast.170, f32[]{:T(128)} %bitcast.169, f32[]{:T(128)} %bitcast.168, f32[]{:T(128)} %bitcast.167, f32[]{:T(128)} %bitcast.166, f32[]{:T(128)} %bitcast.165, f32[]{:T(128)} %bitcast.164, ...), kind=kOutput, calls=%fused_computation.39 | convolution fusion | flops 806846464 | bytes 4194428 | tf_op jit(solution)/shard_map/ij,xjz->xiz/dot_general | solution.py:57
  254.2 21.5 %fusion.16 = f32[32,128,128]{2,1,0:T(8,128)S(1)} fusion(f32[32,128,128]{1,2,0:T(8,128)S(1)} %fusion.32, f32[]{:T(128)} %bitcast.205, f32[]{:T(128)} %bitcast.204, f32[]{:T(128)} %bitcast.203, f32[]{:T(128)} %bitcast.202, f32[]{:T(128)} %bitcast.201, f32[]{:T(128)} %bitcast.200, f32[]{:T(128)} %bitcast.199, f32[]{:T(128)} %bitcast.198, f32[]{:T(128)} %bitcast.197, ...), kind=kOutput, calls=%fused_computation.23 | convolution fusion | flops 806846464 | bytes 4194428 | tf_op jit(solution)/shard_map/ij,xyj->xyi/dot_general | solution.py:58
  275.7 22.7 %fusion.34 = f32[32,128,128]{1,2,0:T(8,128)S(1)} fusion(f32[32,128,128]{2,0,1:T(8,128)S(1)} %fusion.52, f32[]{:T(128)} %bitcast.74, f32[]{:T(128)} %bitcast.73, f32[]{:T(128)} %bitcast.72, f32[]{:T(128)} %bitcast.71, f32[]{:T(128)} %bitcast.70, f32[]{:T(128)} %bitcast.69, f32[]{:T(128)} %bitcast.68, f32[]{:T(128)} %bitcast.67, f32[]{:T(128)} %bitcast.66, ...), kind=kOutput, calls=%fused_computation.41 | convolution fusion | flops 806846464 | bytes 4194428 | tf_op jit(solution)/shard_map/ij,xjz->xiz/dot_general | solution.py:57
  298.5 24.0 %log_multiply_fusion.1 = f32[32,128,128]{2,1,0:T(8,128)} fusion(f32[32,128,128]{2,1,0:T(8,128)S(1)} %fusion.16, f32[32,128,128]{1,2,0:T(8,128)S(1)} %fusion.34, f32[]{:T(128)} %bitcast.109, f32[]{:T(128)} %bitcast, f32[]{:T(128)S(6)} %div.24, f32[]{:T(128)} %bitcast.107, f32[]{:T(128)} %bitcast.106, f32[]{:T(128)} %bitcast.105, f32[]{:T(128)} %bitcast.104, ...), kind=kOutput, calls=%fused_computation.51 | convolution fusion | flops 808943616 | bytes 6291592 | tf_op jit(solution)/shard_map/ij,xyj->xyi/dot_general | solution.py:58
  322.5 96.5 %all-reduce.4.cloned.1.call-done = f32[32,128,128]{2,1,0:T(8,128)} async-done(((f32[32,128,128]{2,1,0:T(8,128)}), f32[32,128,128]{2,1,0:T(8,128)}) %all-reduce.4.cloned.1.call-update) | async-done | bytes 2097168 | tf_op jit(solution)/shard_map/psum | solution.py:97
  428.0 21.3 %fusion.46 = f32[32,128,128]{2,0,1:T(8,128)S(1)} fusion(bf16[62,128,128]{2,1,0:T(8,128)(2,1)S(1)} %pad_maximum_fusion.2, f32[]{:T(128)} %bitcast.140, f32[]{:T(128)} %bitcast.139, f32[]{:T(128)} %bitcast.138, f32[]{:T(128)} %bitcast.137, f32[]{:T(128)} %bitcast.136, f32[]{:T(128)} %bitcast.135, f32[]{:T(128)} %bitcast.134, f32[]{:T(128)} %bitcast.133, ...), kind=kOutput, calls=%fused_computation.65 | convolution fusion | flops 390254784 | bytes 4128892 | tf_op jit(solution)/shard_map/ij,jyz->iyz/dot_general | solution.py:56
  470.7 22.7 %fusion.28 = f32[32,128,128]{1,2,0:T(8,128)S(1)} fusion(f32[32,128,128]{2,0,1:T(8,128)S(1)} %fusion.46, f32[]{:T(128)} %bitcast.172, f32[]{:T(128)} %bitcast.171, f32[]{:T(128)} %bitcast.170, f32[]{:T(128)} %bitcast.169, f32[]{:T(128)} %bitcast.168, f32[]{:T(128)} %bitcast.167, f32[]{:T(128)} %bitcast.166, f32[]{:T(128)} %bitcast.165, f32[]{:T(128)} %bitcast.164, ...), kind=kOutput, calls=%fused_computation.35 | convolution fusion | flops 806846464 | bytes 4194428 | tf_op jit(solution)/shard_map/ij,xjz->xiz/dot_general | solution.py:57
  493.4 21.5 %fusion.12 = f32[32,128,128]{2,1,0:T(8,128)S(1)} fusion(f32[32,128,128]{1,2,0:T(8,128)S(1)} %fusion.28, f32[]{:T(128)} %bitcast.205, f32[]{:T(128)} %bitcast.204, f32[]{:T(128)} %bitcast.203, f32[]{:T(128)} %bitcast.202, f32[]{:T(128)} %bitcast.201, f32[]{:T(128)} %bitcast.200, f32[]{:T(128)} %bitcast.199, f32[]{:T(128)} %bitcast.198, f32[]{:T(128)} %bitcast.197, ...), kind=kOutput, calls=%fused_computation.19 | convolution fusion | flops 806846464 | bytes 4194428 | tf_op jit(solution)/shard_map/ij,xyj->xyi/dot_general | solution.py:58
  514.9 22.6 %fusion.30 = f32[32,128,128]{1,2,0:T(8,128)S(1)} fusion(f32[32,128,128]{2,0,1:T(8,128)S(1)} %fusion.48, f32[]{:T(128)} %bitcast.74, f32[]{:T(128)} %bitcast.73, f32[]{:T(128)} %bitcast.72, f32[]{:T(128)} %bitcast.71, f32[]{:T(128)} %bitcast.70, f32[]{:T(128)} %bitcast.69, f32[]{:T(128)} %bitcast.68, f32[]{:T(128)} %bitcast.67, f32[]{:T(128)} %bitcast.66, ...), kind=kOutput, calls=%fused_computation.37 | convolution fusion | flops 806846464 | bytes 4194428 | tf_op jit(solution)/shard_map/ij,xjz->xiz/dot_general | solution.py:57
  537.5 22.9 %divide_convert_fusion = bf16[32,128,128]{2,1,0:T(8,128)(2,1)S(1)} fusion(f32[32,128,128]{2,1,0:T(8,128)S(1)} %fusion.12, bf16[32,128,128]{2,1,0:T(8,128)(2,1)S(1)} %copy-done.2, f32[32,128,128]{1,2,0:T(8,128)S(1)} %fusion.30, f32[]{:T(128)} %bitcast.109, f32[]{:T(128)} %bitcast, f32[]{:T(128)} %bitcast.107, f32[]{:T(128)} %bitcast.106, f32[]{:T(128)} %bitcast.105, ...), kind=kOutput, calls=%fused_computation.49 | convolution fusion | flops 811040768 | bytes 6291588 | tf_op jit(solution)/shard_map/ij,xyj->xyi/dot_general | solution.py:58
  575.8 21.3 %fusion.42 = f32[32,128,128]{2,0,1:T(8,128)S(1)} fusion(bf16[62,128,128]{2,1,0:T(8,128)(2,1)S(1)} %pad_maximum_fusion.3, f32[]{:T(128)} %bitcast.140, f32[]{:T(128)} %bitcast.139, f32[]{:T(128)} %bitcast.138, f32[]{:T(128)} %bitcast.137, f32[]{:T(128)} %bitcast.136, f32[]{:T(128)} %bitcast.135, f32[]{:T(128)} %bitcast.134, f32[]{:T(128)} %bitcast.133, ...), kind=kOutput, calls=%fused_computation.61 | convolution fusion | flops 390254784 | bytes 4128892 | tf_op jit(solution)/shard_map/ij,jyz->iyz/dot_general | solution.py:56
  597.1 21.3 %fusion.44 = f32[32,128,128]{2,0,1:T(8,128)S(1)} fusion(bf16[62,128,128]{2,1,0:T(8,128)(2,1)S(1)} %pad_maximum_fusion.3, f32[]{:T(128)} %bitcast.32, f32[]{:T(128)} %bitcast.31, f32[]{:T(128)} %bitcast.30, f32[]{:T(128)} %bitcast.29, f32[]{:T(128)} %bitcast.28, f32[]{:T(128)} %bitcast.27, f32[]{:T(128)} %bitcast.26, f32[]{:T(128)} %bitcast.25, ...), kind=kOutput, calls=%fused_computation.63 | convolution fusion | flops 390254784 | bytes 4128892 | tf_op jit(solution)/shard_map/ij,jyz->iyz/dot_general | solution.py:56
  618.5 22.7 %fusion.24 = f32[32,128,128]{1,2,0:T(8,128)S(1)} fusion(f32[32,128,128]{2,0,1:T(8,128)S(1)} %fusion.42, f32[]{:T(128)} %bitcast.172, f32[]{:T(128)} %bitcast.171, f32[]{:T(128)} %bitcast.170, f32[]{:T(128)} %bitcast.169, f32[]{:T(128)} %bitcast.168, f32[]{:T(128)} %bitcast.167, f32[]{:T(128)} %bitcast.166, f32[]{:T(128)} %bitcast.165, f32[]{:T(128)} %bitcast.164, ...), kind=kOutput, calls=%fused_computation.31 | convolution fusion | flops 806846464 | bytes 4194428 | tf_op jit(solution)/shard_map/ij,xjz->xiz/dot_general | solution.py:57
  641.2 21.5 %fusion.8 = f32[32,128,128]{2,1,0:T(8,128)S(1)} fusion(f32[32,128,128]{1,2,0:T(8,128)S(1)} %fusion.24, f32[]{:T(128)} %bitcast.205, f32[]{:T(128)} %bitcast.204, f32[]{:T(128)} %bitcast.203, f32[]{:T(128)} %bitcast.202, f32[]{:T(128)} %bitcast.201, f32[]{:T(128)} %bitcast.200, f32[]{:T(128)} %bitcast.199, f32[]{:T(128)} %bitcast.198, f32[]{:T(128)} %bitcast.197, ...), kind=kOutput, calls=%fused_computation.15 | convolution fusion | flops 806846464 | bytes 4194428 | tf_op jit(solution)/shard_map/ij,xyj->xyi/dot_general | solution.py:58
  662.7 22.5 %fusion.26 = f32[32,128,128]{1,2,0:T(8,128)S(1)} fusion(f32[32,128,128]{2,0,1:T(8,128)S(1)} %fusion.44, f32[]{:T(128)} %bitcast.74, f32[]{:T(128)} %bitcast.73, f32[]{:T(128)} %bitcast.72, f32[]{:T(128)} %bitcast.71, f32[]{:T(128)} %bitcast.70, f32[]{:T(128)} %bitcast.69, f32[]{:T(128)} %bitcast.68, f32[]{:T(128)} %bitcast.67, f32[]{:T(128)} %bitcast.66, ...), kind=kOutput, calls=%fused_computation.33 | convolution fusion | flops 806846464 | bytes 4194428 | tf_op jit(solution)/shard_map/ij,xjz->xiz/dot_general | solution.py:57
  685.2 24.0 %log_multiply_fusion = f32[32,128,128]{2,1,0:T(8,128)} fusion(f32[32,128,128]{2,1,0:T(8,128)S(1)} %fusion.8, f32[32,128,128]{1,2,0:T(8,128)S(1)} %fusion.26, f32[]{:T(128)} %bitcast.109, f32[]{:T(128)} %bitcast, f32[]{:T(128)S(6)} %div.24, f32[]{:T(128)} %bitcast.107, f32[]{:T(128)} %bitcast.106, f32[]{:T(128)} %bitcast.105, f32[]{:T(128)} %bitcast.104, ...), kind=kOutput, calls=%fused_computation.48 | convolution fusion | flops 808943616 | bytes 6291592 | tf_op jit(solution)/shard_map/ij,xyj->xyi/dot_general | solution.py:58
  709.2 92.3 %all-reduce.6.cloned.1.call-done = f32[32,128,128]{2,1,0:T(8,128)} async-done(((f32[32,128,128]{2,1,0:T(8,128)}), f32[32,128,128]{2,1,0:T(8,128)}) %all-reduce.6.cloned.1.call-update) | async-done | bytes 2097168 | tf_op jit(solution)/shard_map/psum | solution.py:97
  (74 shorter events, 115.4 us)
Async XLA Ops:
  6.5 412.5 %all-reduce.4.cloned.1.call-start = ((), (), s32[]{:S(2)}) async-start(), calls=%async_computation | async-start | bytes 4194304 | tf_op jit(solution)/shard_map/psum | solution.py:97
  8.4 30.4 %collective-permute-start.1 = (bf16[8,128,128]{2,1,0:T(8,128)(2,1)}, bf16[8,128,128]{2,1,0:T(8,128)(2,1)}, u32[]{:S(2)}, u32[]{:S(2)}) collective-permute-start(bf16[8,128,128]{2,1,0:T(8,128)(2,1)} %get-tuple-element.13), channel_id=1, source_target_pairs={{4,0},{8,4},{12,8},{16,12},{20,16},{24,20},{28,24},{5,1},{9,5},{13... | collective-permute-start | bytes 786440 | tf_op jit(solution)/shard_map/ppermute | solution.py:22
  9.7 12.4 %copy-start.3 = (f32[1,2,3,31]{3,1,2,0:T(2,128)S(1)}, f32[1,2,3,31]{3,1,2,0:T(2,128)}, u32[]{:S(2)}) copy-start(f32[1,2,3,31]{3,1,2,0:T(2,128)} %param.9) | copy-start | bytes 2236
  9.7 29.1 %collective-permute-start = (bf16[8,128,128]{2,1,0:T(8,128)(2,1)}, bf16[8,128,128]{2,1,0:T(8,128)(2,1)}, u32[]{:S(2)}, u32[]{:S(2)}) collective-permute-start(bf16[8,128,128]{2,1,0:T(8,128)(2,1)} %get-tuple-element.14), channel_id=1, source_target_pairs={{0,4},{4,8},{8,12},{12,16},{16,20},{20,24},{24,28},{1,5},{5,9},{9,... | collective-permute-start | bytes 786440 | tf_op jit(solution)/shard_map/ppermute | solution.py:19
  16.1 14.8 %copy-start.7 = (f32[1,2]{1,0:T(1,128)S(1)}, f32[1,2]{1,0:T(1,128)}, u32[]{:S(2)}) copy-start(f32[1,2]{1,0:T(1,128)} %param.10) | copy-start | bytes 28
  16.1 16.2 %copy-start.4 = (s32[1,3]{1,0:T(1,128)S(1)}, s32[1,3]{1,0:T(1,128)}, u32[]{:S(2)}) copy-start(s32[1,3]{1,0:T(1,128)} %param.11) | copy-start | bytes 40
  16.1 30.4 %collective-permute-start.2 = (bf16[15,128,128]{2,1,0:T(8,128)(2,1)}, bf16[15,128,128]{2,1,0:T(8,128)(2,1)}, u32[]{:S(2)}, u32[]{:S(2)}) collective-permute-start(bf16[15,128,128]{2,1,0:T(8,128)(2,1)} %get-tuple-element.15), channel_id=1, source_target_pairs={{0,4},{4,8},{8,12},{12,16},{16,20},{20,24},{24,28},{1,5},{5,9},{9,... | collective-permute-start | bytes 1474568 | tf_op jit(solution)/shard_map/ppermute | solution.py:19
  20.8 25.7 %collective-permute-start.3 = (bf16[15,128,128]{2,1,0:T(8,128)(2,1)S(1)}, bf16[15,128,128]{2,1,0:T(8,128)(2,1)}, u32[]{:S(2)}, u32[]{:S(2)}) collective-permute-start(bf16[15,128,128]{2,1,0:T(8,128)(2,1)S(1)} %get-tuple-element.16), channel_id=1, source_target_pairs={{4,0},{8,4},{12,8},{16,12},{20,16},{24,20},{28,24},{5,1},{9,5},{13... | collective-permute-start | bytes 1474568 | tf_op jit(solution)/shard_map/ppermute | solution.py:22
  46.5 111.5 %copy-start.1 = (bf16[32,128,128]{2,1,0:T(8,128)(2,1)}, bf16[32,128,128]{2,1,0:T(8,128)(2,1)S(1)}, u32[]{:S(2)}) copy-start(bf16[32,128,128]{2,1,0:T(8,128)(2,1)S(1)} %fusion.66) | copy-start | bytes 3145732
  158.0 27.5 %copy-start.5 = (s32[4]{0:T(128)S(1)}, s32[4]{0:T(128)}, u32[]{:S(2)}) copy-start(s32[4]{0:T(128)} %param.12) | copy-start | bytes 52
  158.0 27.5 %copy-start.6 = (s32[4]{0:T(128)S(1)}, s32[4]{0:T(128)}, u32[]{:S(2)}) copy-start(s32[4]{0:T(128)} %param.13) | copy-start | bytes 52
  181.1 6.5 collective-permute-start.4
  184.2 4.4 collective-permute-start.5
  322.5 96.5 %copy-start = (f32[32,128,128]{2,1,0:T(8,128)S(1)}, f32[32,128,128]{2,1,0:T(8,128)}, u32[]{:S(2)}) copy-start(f32[32,128,128]{2,1,0:T(8,128)} %param.7) | copy-start | bytes 6291460
  322.5 479.1 %all-reduce.6.cloned.1.call-start = ((), (), s32[]{:S(2)}) async-start(), calls=%async_computation.1 | async-start | bytes 4194304 | tf_op jit(solution)/shard_map/psum | solution.py:97
  421.1 3.2 collective-permute-start.6
  422.8 5.0 collective-permute-start.7
  514.9 22.6 %copy-start.2 = (bf16[32,128,128]{2,1,0:T(8,128)(2,1)S(1)}, bf16[32,128,128]{2,1,0:T(8,128)(2,1)}, u32[]{:S(2)}) copy-start(bf16[32,128,128]{2,1,0:T(8,128)(2,1)} %copy-done.1) | copy-start | bytes 3145732
  560.5 12.8 %collective-permute-start.8 = (bf16[15,128,128]{2,1,0:T(8,128)(2,1)S(1)}, bf16[15,128,128]{2,1,0:T(8,128)(2,1)S(1)}, u32[]{:S(2)}, u32[]{:S(2)}) collective-permute-start(bf16[15,128,128]{2,1,0:T(8,128)(2,1)S(1)} %get-tuple-element.7), channel_id=1, source_target_pairs={{0,4},{4,8},{8,12},{12,16},{16,20},{20,24},{24,28},{1,5},{5,9},{9,... | collective-permute-start | bytes 1474568 | tf_op jit(solution)/shard_map/ppermute | solution.py:19
  571.8 3.8 collective-permute-start.9
Sparse Core Ops, SparseCore 0:
  322.6 96.3 all-reduce.3
  709.4 92.1 all-reduce.5
where the time goes:
time: 829 us; the launch traced here: 813 us
  matrix products  532 us (64%)
  waiting for transfers between devices  196 us (24%)
  starting transfers between devices  31 us (4%)
  other arithmetic  22.4 us (3%)
  between operations  19.4 us (2%)
  local copies, waits for them, and re-layouts  12.2 us (1%)
    psum x2, waiting for transfers between devices, on_device(): field = field * jnp.exp(lax.psum(weighted_log, 'view'))  189 us
    dot_general x8, matrix products, blur_block(): jnp.einsum('ij,xjz->xiz', mat_y, part, precision=lax.Precision.HIGHEST)  181 us
    dot_general x8, matrix products, blur_block(): jnp.einsum('ij,xyj->xyi', mat_z, part, precision=lax.Precision.HIGHEST)  180 us
    dot_general x8, matrix products, blur_block(): jnp.einsum('ij,jyz->iyz', mat_x, window, precision=lax.Precision.HIGHEST)  171 us
    ppermute x5, starting transfers between devices, padded(): lax.ppermute(lax.slice_in_dim(block, block.shape[dim] - width, None, axis...  24.6 us
  transfers between devices with their start and end apart: 12, of which 7 were waited for; matrix products, arithmetic and copies ran while one was open for 3% of the time, Pallas kernels for 0%

commit v1 on v0

v1 whole, which is shorter than its diff:
```python
import functools

import jax
import jax.numpy as jnp
from jax import lax
from jax.experimental import pallas as pl
from jax.experimental.pallas import tpu as pltpu
from jax.sharding import PartitionSpec as P

SHIFT_MAX = 8
ROUNDS = 2
HALF_TAPS = 15
HALO = 16
OFFSET = 0.1
GROUP = 16


def halo(block, axis, dim, width):
    count = lax.axis_size(axis)
    forward = [(i, i + 1) for i in range(count - 1)]
    backward = [(target, source) for source, target in forward]
    low = lax.ppermute(
        lax.slice_in_dim(block, block.shape[dim] - width, None, axis=dim), axis, forward
    )
    high = lax.ppermute(lax.slice_in_dim(block, 0, width, axis=dim), axis, backward)
    return low, high


def split(value):
    high = value.astype(jnp.bfloat16)
    low = (value - high.astype(jnp.float32)).astype(jnp.bfloat16)
    return high, low


def dot(a, b):
    return jnp.dot(a, b, preferred_element_type=jnp.float32)


def band(taps, rank, factor, diff, reverse):
    count = taps.shape[2]
    matrix = jnp.zeros(diff.shape, jnp.float32)
    total = jnp.float32(0.0)
    for place in range(count):
        tap = taps[rank, factor, count - 1 - place if reverse else place]
        total = total + tap
        matrix = jnp.where(diff == place, tap, matrix)
    return matrix / jnp.full(diff.shape, total, jnp.float32)


def iota(shape, dim):
    return lax.broadcasted_iota(jnp.int32, shape, dim)


def blur_tables(taps, weight, planes, width, rows, cols, reverse, mat_x, mat_y, mat_z):
    half = HALF_TAPS
    weight_sum = weight[0] + weight[1]
    shape = (planes, 4 * width)
    part = iota(shape, 1) // width
    diff = iota(shape, 1) % width - iota(shape, 0) - (HALO - half)
    for rank in range(2):
        scale = jnp.full(shape, weight[rank], jnp.float32) / jnp.full(shape, weight_sum, jnp.float32)
        full = band(taps, rank, 0, diff, reverse) * scale
        high = full.astype(jnp.bfloat16).astype(jnp.float32)
        mixed = jnp.where(part < 2, high, jnp.where(part == 2, full - high, 0.0))
        mat_x[rank * planes : (rank + 1) * planes, :] = mixed.astype(jnp.bfloat16)
        shape_y = (rows, rows)
        high, low = split(
            band(taps, rank, 1, iota(shape_y, 1) - iota(shape_y, 0) + half, reverse)
        )
        mat_y[:rows, rank * rows : (rank + 1) * rows] = high
        mat_y[rows:, rank * rows : (rank + 1) * rows] = low
        shape_z = (cols, cols)
        high, low = split(
            band(taps, rank, 2, iota(shape_z, 0) - iota(shape_z, 1) + half, reverse)
        )
        for copy in range(2):
            mat_z[rank, copy * cols : (copy + 1) * cols, :cols] = high
            mat_z[rank, copy * cols : (copy + 1) * cols, cols:] = low


def blur(window, middle, mat_x, mat_y, mat_z, planes, width, rows, cols, finish):
    def first(step, carry):
        base = step * GROUP
        parts = []
        for k in range(GROUP // 2):
            sides = []
            for side in range(2):
                y = base + 2 * k + side
                high, low = split(window[pl.ds(y, width, stride=rows), :])
                sides.append(jnp.concatenate([high, low, high], axis=0))
            both = dot(mat_x[:, : 3 * width], jnp.concatenate(sides, axis=1))
            parts.append(both[:, :cols])
            parts.append(both[:, cols:])
        for rank in range(2):
            stack = jnp.concatenate(
                [p[rank * planes : (rank + 1) * planes] for p in parts], axis=0
            )
            high, low = split(stack)
            both = dot(jnp.concatenate([high, low], axis=1), mat_z[rank])
            result = both[:, :cols] + both[:, cols:]
            for k in range(GROUP):
                middle[pl.ds(rank * planes * rows + base + k, planes, stride=rows), :] = result[
                    k * planes : (k + 1) * planes
                ]
        return carry

    lax.fori_loop(0, rows // GROUP, first, 0)

    def second(step, carry):
        x = 2 * step
        highs, lows = [], []
        for side in range(2):
            data = [
                middle[pl.ds(pl.multiple_of((rank * planes + x + side) * rows, 8), rows), :]
                for rank in range(2)
            ]
            high, low = split(jnp.concatenate(data, axis=0))
            highs.append(high)
            lows.append(low)
        both = dot(mat_y[...], jnp.concatenate(highs, axis=1))
        result = both[:rows] + both[rows:]
        result = result + dot(mat_y[:rows, :], jnp.concatenate(lows, axis=1))
        finish(x, result[:, :cols])
        finish(x + 1, result[:, cols:])
        return carry

    lax.fori_loop(0, planes // 2, second, 0)


def load_window(low, own, high, window, planes, rows, cols):
    size = HALO * rows
    window[:size, :] = low[...].astype(jnp.float32).reshape(size, cols)
    window[size : size + planes * rows, :] = own[...].reshape(planes * rows, cols)
    window[size + planes * rows :, :] = high[...].astype(jnp.float32).reshape(size, cols)


def forward_kernel(taps, weight, low, own, high, registered, out, window, middle, mx, my, mz):
    planes, rows, cols = own.shape
    width = planes + 2 * HALO
    blur_tables(taps, weight, planes, width, rows, cols, False, mx, my, mz)
    load_window(low, own, high, window, planes, rows, cols)

    def finish(x, value):
        out[x] = (registered[x].astype(jnp.float32) + OFFSET) / (value + OFFSET)

    blur(window, middle, mx, my, mz, planes, width, rows, cols, finish)


def backward_kernel(
    taps, weight, first, count, low, own, high, out, window, middle, mx, my, mz
):
    planes, rows, cols = own.shape
    width = planes + 2 * HALO
    blur_tables(taps, weight, planes, width, rows, cols, True, mx, my, mz)
    load_window(low, own, high, window, planes, rows, cols)
    view = lax.axis_index("view")
    block = lax.axis_index("blk")
    covered = jnp.float32(0.0)
    owned = jnp.float32(0.0)
    for slot in range(first.shape[0]):
        inside = (block >= first[slot]) & (block < first[slot] + count[slot])
        covered = covered + jnp.where(inside, 1.0, 0.0)
        owned = owned + jnp.where(inside & (view == slot), 1.0, 0.0)
    share = jnp.full((rows, cols), owned, jnp.float32) / jnp.full((rows, cols), covered, jnp.float32)

    def finish(x, value):
        out[x] = share * jnp.log(value)

    blur(window, middle, mx, my, mz, planes, width, rows, cols, finish)


def call(kernel, scalars, arrays, shape):
    planes, rows, cols = shape
    width = planes + 2 * HALO
    return pl.pallas_call(
        kernel,
        out_shape=jax.ShapeDtypeStruct(shape, jnp.float32),
        in_specs=[pl.BlockSpec(memory_space=pltpu.SMEM)] * len(scalars)
        + [pl.BlockSpec(memory_space=pltpu.VMEM)] * len(arrays),
        out_specs=pl.BlockSpec(memory_space=pltpu.VMEM),
        scratch_shapes=[
            pltpu.VMEM((width * rows, cols), jnp.float32),
            pltpu.VMEM((2 * planes * rows, cols), jnp.float32),
            pltpu.VMEM((2 * planes, 4 * width), jnp.bfloat16),
            pltpu.VMEM((2 * rows, 2 * rows), jnp.bfloat16),
            pltpu.VMEM((2, 2 * cols, 2 * cols), jnp.bfloat16),
        ],
        compiler_params=pltpu.CompilerParams(vmem_limit_bytes=40 * 2**20),
        cost_estimate=pl.CostEstimate(
            flops=12 * planes * rows * cols * 3 * cols,
            bytes_accessed=12 * planes * rows * cols,
            transcendentals=0,
        ),
    )(*scalars, *arrays)


def on_device(estimate, observed, psf_taps, psf_weight, shifts, cover_first, cover_count):
    planes, rows, cols = estimate.shape
    taps, weight = psf_taps[0], psf_weight[0]
    field_low, field_high = halo(estimate.astype(jnp.bfloat16), "blk", 0, HALO)
    low, high = halo(observed[0], "blk", 0, SHIFT_MAX)
    extended = jnp.concatenate([low, observed[0], high], axis=0)
    extended = jnp.pad(extended, ((0, 0), (SHIFT_MAX, SHIFT_MAX), (SHIFT_MAX, SHIFT_MAX)))
    start = (SHIFT_MAX + shifts[0, 0], SHIFT_MAX + shifts[0, 1], SHIFT_MAX + shifts[0, 2])
    registered = lax.dynamic_slice(extended, start, (planes, rows, cols))
    field = estimate
    for step in range(ROUNDS):
        if step:
            field_low, field_high = halo(field.astype(jnp.bfloat16), "blk", 0, HALO)
        ratio = call(
            forward_kernel,
            (taps, weight),
            (field_low, field, field_high, registered),
            estimate.shape,
        )
        ratio_low, ratio_high = halo(ratio.astype(jnp.bfloat16), "blk", 0, HALO)
        weighted_log = call(
            backward_kernel,
            (taps, weight, cover_first, cover_count),
            (ratio_low, ratio, ratio_high),
            estimate.shape,
        )
        field = field * jnp.exp(lax.psum(weighted_log, "view"))
    return field


def solution(mesh):
    placed = (
        P("blk", None, None),
        P("view", "blk", None, None),
        P("view", None, None, None),
        P("view", None),
        P("view", None),
        P(),
        P(),
    )
    return jax.shard_map(
        on_device, mesh=mesh, in_specs=placed, out_specs=P("blk", None, None), check_vma=False
    )
```

time: 829 us -> 332 us (0.40)
  the two profiles are of different devices: /device:TPU:0 before, /device:TPU:4 now
where the time goes in v1:
time: 332 us; the launch traced here: 330 us
  waiting for transfers between devices  207 us (62%)
  Pallas kernels  54.8 us (17%)
  starting transfers between devices  27 us (8%)
  other arithmetic  18.5 us (6%)
  between operations  17.4 us (5%)
  local copies, waits for them, and re-layouts  5.02 us (2%)
    psum x2, waiting for transfers between devices, on_device(): field = field * jnp.exp(lax.psum(weighted_log, 'view'))  177 us
    pallas_call x4, Pallas kernels, call(): pl.pallas_call(kernel, out_shape=jax.ShapeDtypeStruct(shape, jnp.float32)...  54.8 us
    ppermute x5, waiting for transfers between devices, halo(): lax.ppermute(lax.slice_in_dim(block, 0, width, axis=dim), axis, backward)  25.4 us
    ppermute x5, starting transfers between devices, halo(): lax.ppermute(lax.slice_in_dim(block, 0, width, axis=dim), axis, backward)  16.7 us
    ppermute x5, starting transfers between devices, halo(): lax.ppermute(lax.slice_in_dim(block, block.shape[dim] - width, None, axis...  10.3 us
    concatenate x1, other arithmetic, on_device(): extended = jnp.concatenate([low, observed[0], high], axis=0)  7.8 us
  transfers between devices with their start and end apart: 12, of which 7 were waited for; matrix products, arithmetic and copies ran while one was open for 4% of the time, Pallas kernels for 0%

profile of v1, /device:TPU:4, one launch (start us, length us, event | category | flops | bytes accessed | tf_op | source)
XLA Modules:
  0.0 329.9 jit_solution(2063059595964410567)
XLA Ops:
  7.6 2.8 collective-permute-start.3
  10.4 1.9 collective-permute-start.2
  15.2 4.7 %collective-permute-start.1 = (bf16[16,128,128]{2,1,0:T(8,128)(2,1)}, bf16[16,128,128]{2,1,0:T(8,128)(2,1)}, u32[]{:S(2)}, u32[]{:S(2)}) collective-permute-start(bf16[16,128,128]{2,1,0:T(8,128)(2,1)} %get-tuple-element.15), channel_id=1, source_target_pairs={{4,0},{8,4},{12,8},{16,12},{20,16},{24,20},{28,24},{5,1},{9,5},{13... | collective-permute-start | bytes 1572872 | tf_op jit(solution)/shard_map/ppermute | solution.py:25
  19.8 1.9 collective-permute-start
  21.8 2.7 iota_compare_fusion
  29.6 7.8 %fusion.10.registered = bf16[32,128,128]{2,1,0:T(8,128)(2,1)S(1)} fusion(s32[]{:T(128)S(6)} %select_n.9, s32[]{:T(128)S(6)} %select_n.10, s32[]{:T(128)S(6)} %select_n.11, bf16[8,128,128]{2,1,0:T(8,128)(2,1)} %copy-done.5, bf16[32,128,128]{2,1,0:T(8,128)(2,1)} %bitcast.23, pred[48,144,144]{2,1,0:T(8,128)(4,1)} %get-tuple-element.20, ...), kind=kLoop, calls=%fused_computation.20 | loop fusion | flops 12582912 | bytes 3672576 | tf_op jit(solution)/shard_map/concatenate | solution.py:202
  37.4 13.8 %shard_map.73.own = f32[32,128,128]{2,1,0:T(8,128)S(1)} custom-call(f32[2,3,31]{2,1,0:T(4,128)S(1)} %bitcast.15, f32[2]{0:T(128)S(1)} %bitcast.19, bf16[16,128,128]{2,1,0:T(8,128)(2,1)} %collective-permute-done.low, f32[32,128,128]{2,1,0:T(8,128)S(1)} %copy-done, bf16[16,128,128]{2,1,0:T(8,128)(2,1)} %collective-permute-done.1.high, ...), custom_call_target="tpu_custom_call" | custom-call | flops 2415919104 | bytes 6291456 | tf_op jit(solution)/shard_map/pallas_call | solution.py:175
  51.5 4.5 %collective-permute-start.5 = (bf16[16,128,128]{2,1,0:T(8,128)(2,1)S(1)}, bf16[16,128,128]{2,1,0:T(8,128)(2,1)S(1)}, u32[]{:S(2)}, u32[]{:S(2)}) collective-permute-start(bf16[16,128,128]{2,1,0:T(8,128)(2,1)S(1)} %get-tuple-element.11), channel_id=1, source_target_pairs={{4,0},{8,4},{12,8},{16,12},{20,16},{24,20},{28,24},{5,1},{9,5},{13... | collective-permute-start | bytes 1572872 | tf_op jit(solution)/shard_map/ppermute | solution.py:25
  56.1 2.1 collective-permute-start.4
  58.2 10.0 %collective-permute-done.5.high = bf16[16,128,128]{2,1,0:T(8,128)(2,1)S(1)} collective-permute-done((bf16[16,128,128]{2,1,0:T(8,128)(2,1)S(1)}, bf16[16,128,128]{2,1,0:T(8,128)(2,1)S(1)}, u32[]{:S(2)}, u32[]{:S(2)}) %collective-permute-start.5) | collective-permute-done | bytes 524320 | tf_op jit(solution)/shard_map/ppermute | solution.py:25
  68.2 14.5 %shard_map.74 = f32[32,128,128]{2,1,0:T(8,128)} custom-call(f32[2,3,31]{2,1,0:T(4,128)S(1)} %bitcast.16, f32[2]{0:T(128)S(1)} %bitcast.20, s32[4]{0:T(128)S(1)} %copy-done.3, s32[4]{0:T(128)S(1)} %copy-done.4, bf16[16,128,128]{2,1,0:T(8,128)(2,1)S(1)} %collective-permute-done.4.low, f32[32,128,128]{2,1,0:T(8,128)S(1)} %shard_map.73.own, ...), custom_call_target="tpu_custom_call" | custom-call | flops 2415919104 | bytes 6291456 | tf_op jit(solution)/shard_map/pallas_call | solution.py:175
  82.8 89.1 %all-reduce.4.cloned.1.call-done = f32[32,128,128]{2,1,0:T(8,128)} async-done(((f32[32,128,128]{2,1,0:T(8,128)}), f32[32,128,128]{2,1,0:T(8,128)}) %all-reduce.4.cloned.1.call-update) | async-done | bytes 2097168 | tf_op jit(solution)/shard_map/psum | solution.py:223
  171.9 2.7 fusion.17
  174.6 2.8 collective-permute-start.7
  177.4 1.9 collective-permute-start.6
  179.4 8.4 %collective-permute-done.7.high = bf16[16,128,128]{2,1,0:T(8,128)(2,1)S(1)} collective-permute-done((bf16[16,128,128]{2,1,0:T(8,128)(2,1)S(1)}, bf16[16,128,128]{2,1,0:T(8,128)(2,1)S(1)}, u32[]{:S(2)}, u32[]{:S(2)}) %collective-permute-start.7) | collective-permute-done | bytes 524320 | tf_op jit(solution)/shard_map/ppermute | solution.py:25
  187.7 3.0 collective-permute-done.6.low
  190.8 13.2 %shard_map.75.own = f32[32,128,128]{2,1,0:T(8,128)S(1)} custom-call(f32[2,3,31]{2,1,0:T(4,128)S(1)} %bitcast.17, f32[2]{0:T(128)S(1)} %bitcast.21, bf16[16,128,128]{2,1,0:T(8,128)(2,1)S(1)} %collective-permute-done.6.low, f32[32,128,128]{2,1,0:T(8,128)S(1)} %get-tuple-element.6.own, bf16[16,128,128]{2,1,0:T(8,128)(2,1)S(1)} %collective-permute-done.7.high, ...), custom_call_target="tpu_custom_call" | custom-call | flops 2415919104 | bytes 6291456 | tf_op jit(solution)/shard_map/pallas_call | solution.py:175
  206.1 2.4 collective-permute-start.8
  208.5 7.0 %collective-permute-done.9.high = bf16[16,128,128]{2,1,0:T(8,128)(2,1)S(1)} collective-permute-done((bf16[16,128,128]{2,1,0:T(8,128)(2,1)S(1)}, bf16[16,128,128]{2,1,0:T(8,128)(2,1)S(1)}, u32[]{:S(2)}, u32[]{:S(2)}) %collective-permute-start.9) | collective-permute-done | bytes 524320 | tf_op jit(solution)/shard_map/ppermute | solution.py:25
  215.6 2.0 collective-permute-done.8.low
  217.5 13.2 %shard_map.76 = f32[32,128,128]{2,1,0:T(8,128)S(1)} custom-call(f32[2,3,31]{2,1,0:T(4,128)S(1)} %bitcast.18, f32[2]{0:T(128)S(1)} %bitcast.22, s32[4]{0:T(128)S(1)} %copy-done.3, s32[4]{0:T(128)S(1)} %copy-done.4, bf16[16,128,128]{2,1,0:T(8,128)(2,1)S(1)} %collective-permute-done.8.low, f32[32,128,128]{2,1,0:T(8,128)S(1)} %shard_map.75.own, ...), custom_call_target="tpu_custom_call" | custom-call | flops 2415919104 | bytes 6291456 | tf_op jit(solution)/shard_map/pallas_call | solution.py:175
  232.1 87.7 %all-reduce.6.cloned.1.call-done = f32[32,128,128]{2,1,0:T(8,128)} async-done(((f32[32,128,128]{2,1,0:T(8,128)}), f32[32,128,128]{2,1,0:T(8,128)}) %all-reduce.6.cloned.1.call-update) | async-done | bytes 2097168 | tf_op jit(solution)/shard_map/psum | solution.py:223
  319.9 3.2 exponential_multiply_fusion
  (36 shorter events, 9.1 us)
Async XLA Ops:
  6.5 165.3 %all-reduce.4.cloned.1.call-start = ((), (), s32[]{:S(2)}) async-start(), calls=%async_computation | async-start | bytes 4194304 | tf_op jit(solution)/shard_map/psum | solution.py:223
  7.6 21.2 %collective-permute-start.3 = (bf16[8,128,128]{2,1,0:T(8,128)(2,1)S(1)}, bf16[8,128,128]{2,1,0:T(8,128)(2,1)S(1)}, u32[]{:S(2)}, u32[]{:S(2)}) collective-permute-start(bf16[8,128,128]{2,1,0:T(8,128)(2,1)S(1)} %get-tuple-element.13), channel_id=1, source_target_pairs={{4,0},{8,4},{12,8},{16,12},{20,16},{24,20},{28,24},{5,1},{9,5},{13... | collective-permute-start | bytes 786440 | tf_op jit(solution)/shard_map/ppermute | solution.py:25
  10.4 18.4 %collective-permute-start.2 = (bf16[8,128,128]{2,1,0:T(8,128)(2,1)S(1)}, bf16[8,128,128]{2,1,0:T(8,128)(2,1)S(1)}, u32[]{:S(2)}, u32[]{:S(2)}) collective-permute-start(bf16[8,128,128]{2,1,0:T(8,128)(2,1)S(1)} %get-tuple-element.14), channel_id=1, source_target_pairs={{0,4},{4,8},{8,12},{12,16},{16,20},{20,24},{24,28},{1,5},{5,9},{9,... | collective-permute-start | bytes 786440 | tf_op jit(solution)/shard_map/ppermute | solution.py:22
  15.2 9.3 %copy-start.6 = (s32[1,3]{1,0:T(1,128)S(1)}, s32[1,3]{1,0:T(1,128)}, u32[]{:S(2)}) copy-start(s32[1,3]{1,0:T(1,128)} %param.11) | copy-start | bytes 40
  15.2 13.6 %copy-start.7 = (f32[1,2,3,31]{3,1,2,0:T(2,128)S(1)}, f32[1,2,3,31]{3,1,2,0:T(2,128)}, u32[]{:S(2)}) copy-start(f32[1,2,3,31]{3,1,2,0:T(2,128)} %param.9) | copy-start | bytes 2236
  15.2 22.2 %collective-permute-start.1 = (bf16[16,128,128]{2,1,0:T(8,128)(2,1)}, bf16[16,128,128]{2,1,0:T(8,128)(2,1)}, u32[]{:S(2)}, u32[]{:S(2)}) collective-permute-start(bf16[16,128,128]{2,1,0:T(8,128)(2,1)} %get-tuple-element.15), channel_id=1, source_target_pairs={{4,0},{8,4},{12,8},{16,12},{20,16},{24,20},{28,24},{5,1},{9,5},{13... | collective-permute-start | bytes 1572872 | tf_op jit(solution)/shard_map/ppermute | solution.py:25
  19.8 17.5 %collective-permute-start = (bf16[16,128,128]{2,1,0:T(8,128)(2,1)}, bf16[16,128,128]{2,1,0:T(8,128)(2,1)}, u32[]{:S(2)}, u32[]{:S(2)}) collective-permute-start(bf16[16,128,128]{2,1,0:T(8,128)(2,1)} %get-tuple-element.16), channel_id=1, source_target_pairs={{0,4},{4,8},{8,12},{12,16},{16,20},{20,24},{24,28},{1,5},{5,9},{9,... | collective-permute-start | bytes 1572872 | tf_op jit(solution)/shard_map/ppermute | solution.py:22
  24.5 12.9 %copy-start = (f32[32,128,128]{2,1,0:T(8,128)S(1)}, f32[32,128,128]{2,1,0:T(8,128)}, u32[]{:S(2)}) copy-start(f32[32,128,128]{2,1,0:T(8,128)} %own.1) | copy-start | bytes 6291460
  24.5 12.9 %copy-start.2 = (f32[1,2]{1,0:T(1,128)S(1)}, f32[1,2]{1,0:T(1,128)}, u32[]{:S(2)}) copy-start(f32[1,2]{1,0:T(1,128)} %param.10) | copy-start | bytes 28
  28.9 0.7 copy-start.5
  51.2 17.0 %copy-start.3 = (s32[4]{0:T(128)S(1)}, s32[4]{0:T(128)}, u32[]{:S(2)}) copy-start(s32[4]{0:T(128)} %first.3) | copy-start | bytes 52
  51.2 17.0 %copy-start.4 = (s32[4]{0:T(128)S(1)}, s32[4]{0:T(128)}, u32[]{:S(2)}) copy-start(s32[4]{0:T(128)} %count.3) | copy-start | bytes 52
  51.5 16.7 %collective-permute-start.5 = (bf16[16,128,128]{2,1,0:T(8,128)(2,1)S(1)}, bf16[16,128,128]{2,1,0:T(8,128)(2,1)S(1)}, u32[]{:S(2)}, u32[]{:S(2)}) collective-permute-start(bf16[16,128,128]{2,1,0:T(8,128)(2,1)S(1)} %get-tuple-element.11), channel_id=1, source_target_pairs={{4,0},{8,4},{12,8},{16,12},{20,16},{24,20},{28,24},{5,1},{9,5},{13... | collective-permute-start | bytes 1572872 | tf_op jit(solution)/shard_map/ppermute | solution.py:25
  56.1 12.1 %collective-permute-start.4 = (bf16[16,128,128]{2,1,0:T(8,128)(2,1)S(1)}, bf16[16,128,128]{2,1,0:T(8,128)(2,1)S(1)}, u32[]{:S(2)}, u32[]{:S(2)}) collective-permute-start(bf16[16,128,128]{2,1,0:T(8,128)(2,1)S(1)} %get-tuple-element.12), channel_id=1, source_target_pairs={{0,4},{4,8},{8,12},{12,16},{16,20},{20,24},{24,28},{1,5},{5,9},{9,... | collective-permute-start | bytes 1572872 | tf_op jit(solution)/shard_map/ppermute | solution.py:22
  82.7 237.1 %all-reduce.6.cloned.1.call-start = ((), (), s32[]{:S(2)}) async-start(), calls=%async_computation.1 | async-start | bytes 4194304 | tf_op jit(solution)/shard_map/psum | solution.py:223
  174.6 13.1 %collective-permute-start.7 = (bf16[16,128,128]{2,1,0:T(8,128)(2,1)S(1)}, bf16[16,128,128]{2,1,0:T(8,128)(2,1)S(1)}, u32[]{:S(2)}, u32[]{:S(2)}) collective-permute-start(bf16[16,128,128]{2,1,0:T(8,128)(2,1)S(1)} %get-tuple-element.9), channel_id=1, source_target_pairs={{4,0},{8,4},{12,8},{16,12},{20,16},{24,20},{28,24},{5,1},{9,5},{13... | collective-permute-start | bytes 1572872 | tf_op jit(solution)/shard_map/ppermute | solution.py:25
  177.4 13.3 %collective-permute-start.6 = (bf16[16,128,128]{2,1,0:T(8,128)(2,1)S(1)}, bf16[16,128,128]{2,1,0:T(8,128)(2,1)S(1)}, u32[]{:S(2)}, u32[]{:S(2)}) collective-permute-start(bf16[16,128,128]{2,1,0:T(8,128)(2,1)S(1)} %get-tuple-element.10), channel_id=1, source_target_pairs={{0,4},{4,8},{8,12},{12,16},{16,20},{20,24},{24,28},{1,5},{5,9},{9,... | collective-permute-start | bytes 1572872 | tf_op jit(solution)/shard_map/ppermute | solution.py:22
  204.2 11.4 %collective-permute-start.9 = (bf16[16,128,128]{2,1,0:T(8,128)(2,1)S(1)}, bf16[16,128,128]{2,1,0:T(8,128)(2,1)S(1)}, u32[]{:S(2)}, u32[]{:S(2)}) collective-permute-start(bf16[16,128,128]{2,1,0:T(8,128)(2,1)S(1)} %get-tuple-element.7), channel_id=1, source_target_pairs={{4,0},{8,4},{12,8},{16,12},{20,16},{24,20},{28,24},{5,1},{9,5},{13... | collective-permute-start | bytes 1572872 | tf_op jit(solution)/shard_map/ppermute | solution.py:25
  206.1 11.4 %collective-permute-start.8 = (bf16[16,128,128]{2,1,0:T(8,128)(2,1)S(1)}, bf16[16,128,128]{2,1,0:T(8,128)(2,1)S(1)}, u32[]{:S(2)}, u32[]{:S(2)}) collective-permute-start(bf16[16,128,128]{2,1,0:T(8,128)(2,1)S(1)} %get-tuple-element.8), channel_id=1, source_target_pairs={{0,4},{4,8},{8,12},{12,16},{16,20},{20,24},{24,28},{1,5},{5,9},{9,... | collective-permute-start | bytes 1572872 | tf_op jit(solution)/shard_map/ppermute | solution.py:22
  230.8 1.3 copy-start.1
Sparse Core Ops, SparseCore 0:
  82.9 88.9 all-reduce.3
  232.2 87.5 all-reduce.5

commit v2 on v1

--- a/solution.py
+++ b/solution.py
@@ -1,4 +1,4 @@
-import functools
+import math
 
 import jax
 import jax.numpy as jnp
@@ -13,6 +13,10 @@
 HALO = 16
 OFFSET = 0.1
 GROUP = 16
+CHUNKS = 4
+KNEE = 0.05
+LIMIT = 24.0
+UNIT = math.log(1.0 + LIMIT / KNEE) / 32767.0
 
 
 def halo(block, axis, dim, width):
@@ -78,7 +82,7 @@
             mat_z[rank, copy * cols : (copy + 1) * cols, cols:] = low
 
 
-def blur(window, middle, mat_x, mat_y, mat_z, planes, width, rows, cols, finish):
+def blur_xz(window, middle, mat_x, mat_z, planes, width, rows, cols):
     def first(step, carry):
         base = step * GROUP
         parts = []
@@ -106,8 +110,10 @@
 
     lax.fori_loop(0, rows // GROUP, first, 0)
 
+
+def blur_y(middle, mat_y, planes, rows, cols, start, number, finish):
     def second(step, carry):
-        x = 2 * step
+        x = start + 2 * step
         highs, lows = [], []
         for side in range(2):
             data = [
@@ -120,11 +126,11 @@
         both = dot(mat_y[...], jnp.concatenate(highs, axis=1))
         result = both[:rows] + both[rows:]
         result = result + dot(mat_y[:rows, :], jnp.concatenate(lows, axis=1))
-        finish(x, result[:, :cols])
-        finish(x + 1, result[:, cols:])
+        finish(2 * step, result[:, :cols])
+        finish(2 * step + 1, result[:, cols:])
         return carry
 
-    lax.fori_loop(0, planes // 2, second, 0)
+    lax.fori_loop(0, number // 2, second, 0)
 
 
 def load_window(low, own, high, window, planes, rows, cols):
@@ -143,18 +149,41 @@
     def finish(x, value):
         out[x] = (registered[x].astype(jnp.float32) + OFFSET) / (value + OFFSET)
 
-    blur(window, middle, mx, my, mz, planes, width, rows, cols, finish)
+    blur_xz(window, middle, mx, mz, planes, width, rows, cols)
+    blur_y(middle, my, planes, rows, cols, 0, planes, finish)
+
+
+def encode(value):
+    size = jnp.log(1.0 + jnp.abs(value) * (1.0 / KNEE)) * (1.0 / UNIT) + 0.5
+    size = jnp.minimum(size, 32767.0)
+    return jnp.where(value < 0.0, -size, size).astype(jnp.int32).astype(jnp.int16)
+
+
+def decode(code):
+    value = code.astype(jnp.int32).astype(jnp.float32)
+    size = KNEE * (jnp.exp(UNIT * jnp.abs(value)) - 1.0)
+    return jnp.where(value < 0.0, -size, size)
 
 
 def backward_kernel(
-    taps, weight, first, count, low, own, high, out, window, middle, mx, my, mz
+    taps, weight, first, count, low, own, high, field, out, window, middle, mx, my, mz,
+    mine, send, recv, send_sems, recv_sems,
 ):
     planes, rows, cols = own.shape
     width = planes + 2 * HALO
+    view = lax.axis_index("view")
+    block = lax.axis_index("blk")
+    side = lax.rem(view, 2)
+    partner = view + 1 - 2 * side
+    across = lax.rem(view + 2, 4)
+    barrier = pltpu.get_barrier_semaphore()
+    for other in (partner, across):
+        pl.semaphore_signal(
+            barrier, inc=1, device_id={"view": other}, device_id_type=pl.DeviceIdType.MESH
+        )
+
     blur_tables(taps, weight, planes, width, rows, cols, True, mx, my, mz)
     load_window(low, own, high, window, planes, rows, cols)
-    view = lax.axis_index("view")
-    block = lax.axis_index("blk")
     covered = jnp.float32(0.0)
     owned = jnp.float32(0.0)
     for slot in range(first.shape[0]):
@@ -163,13 +192,86 @@
         owned = owned + jnp.where(inside & (view == slot), 1.0, 0.0)
     share = jnp.full((rows, cols), owned, jnp.float32) / jnp.full((rows, cols), covered, jnp.float32)
 
-    def finish(x, value):
-        out[x] = share * jnp.log(value)
-
-    blur(window, middle, mx, my, mz, planes, width, rows, cols, finish)
-
-
-def call(kernel, scalars, arrays, shape):
+    blur_xz(window, middle, mx, mz, planes, width, rows, cols)
+    pl.semaphore_wait(barrier, 2)
+
+    half = planes // (2 * CHUNKS)
+
+    def copy(stage, chunk):
+        return pltpu.make_async_remote_copy(
+            src_ref=send.at[stage, chunk],
+            dst_ref=recv.at[stage, chunk],
+            send_sem=send_sems.at[stage, chunk],
+            recv_sem=recv_sems.at[stage, chunk],
+            device_id={"view": across if stage == 1 else partner},
+            device_id_type=pl.DeviceIdType.MESH,
+        )
+
+    def produce(chunk):
+        base = chunk * 2 * half
+
+        def give(place, value):
+            send[0, chunk, place] = encode(share * jnp.log(value))
+
+        blur_y(middle, my, planes, rows, cols, base + (1 - side) * half, half, give)
+        copy(0, chunk).start()
+
+        def keep(place, value):
+            mine[chunk, place] = share * jnp.log(value)
+
+        blur_y(middle, my, planes, rows, cols, base + side * half, half, keep)
+
+    def add_pair(chunk):
+        copy(0, chunk).wait_recv()
+
+        def body(place, carry):
+            send[1, chunk, place] = encode(mine[chunk, place] + decode(recv[0, chunk, place]))
+            return carry
+
+        lax.fori_loop(0, half, body, 0)
+        copy(1, chunk).start()
+
+    def update(chunk, place, which, code):
+        x = chunk * 2 * half + which * half + place
+        out[x] = field[x] * jnp.exp(decode(code))
+
+    def add_across(chunk):
+        copy(1, chunk).wait_recv()
+
+        def body(place, carry):
+            total = encode(decode(send[1, chunk, place]) + decode(recv[1, chunk, place]))
+            send[2, chunk, place] = total
+            update(chunk, place, side, total)
+            return carry
+
+        lax.fori_loop(0, half, body, 0)
+        copy(2, chunk).start()
+
+    def take(chunk):
+        copy(2, chunk).wait_recv()
+
+        def body(place, carry):
+            update(chunk, place, 1 - side, recv[2, chunk, place])
+            return carry
+
+        lax.fori_loop(0, half, body, 0)
+
+    for chunk in range(CHUNKS):
+        produce(chunk)
+        if chunk:
+            add_pair(chunk - 1)
+    add_pair(CHUNKS - 1)
+    for chunk in range(CHUNKS):
+        add_across(chunk)
+        if chunk:
+            take(chunk - 1)
+    take(CHUNKS - 1)
+    for stage in range(3):
+        for chunk in range(CHUNKS):
+            copy(stage, chunk).wait_send()
+
+
+def call(kernel, scalars, arrays, shape, scratch=(), **params):
     planes, rows, cols = shape
     width = planes + 2 * HALO
     return pl.pallas_call(
@@ -184,8 +286,9 @@
             pltpu.VMEM((2 * planes, 4 * width), jnp.bfloat16),
             pltpu.VMEM((2 * rows, 2 * rows), jnp.bfloat16),
             pltpu.VMEM((2, 2 * cols, 2 * cols), jnp.bfloat16),
+            *scratch,
         ],
-        compiler_params=pltpu.CompilerParams(vmem_limit_bytes=40 * 2**20),
+        compiler_params=pltpu.CompilerParams(vmem_limit_bytes=40 * 2**20, **params),
         cost_estimate=pl.CostEstimate(
             flops=12 * planes * rows * cols * 3 * cols,
             bytes_accessed=12 * planes * rows * cols,
@@ -214,13 +317,22 @@
             estimate.shape,
         )
         ratio_low, ratio_high = halo(ratio.astype(jnp.bfloat16), "blk", 0, HALO)
-        weighted_log = call(
+        chunk = (CHUNKS, planes // (2 * CHUNKS), rows, cols)
+        field = call(
             backward_kernel,
             (taps, weight, cover_first, cover_count),
-            (ratio_low, ratio, ratio_high),
+            (ratio_low, ratio, ratio_high, field),
             estimate.shape,
-        )
-        field = field * jnp.exp(lax.psum(weighted_log, "view"))
+            (
+                pltpu.VMEM(chunk, jnp.float32),
+                pltpu.VMEM((3, *chunk), jnp.int16),
+                pltpu.VMEM((3, *chunk), jnp.int16),
+                pltpu.SemaphoreType.DMA((3, CHUNKS)),
+                pltpu.SemaphoreType.DMA((3, CHUNKS)),
+            ),
+            collective_id=0,
+            has_side_effects=True,
+        )
     return field
 
 

time: 332 us -> 202 us (0.61)
  waiting for transfers between devices: 207 us -> 27.9 us
  Pallas kernels: 54.8 us -> 124 us
  between operations: 17.4 us -> 4.01 us
  other arithmetic: 18.5 us -> 12.7 us
    psum x2 -> x0, waiting for transfers between devices: 177 us -> none  [on_device(): field = field * jnp.exp(lax.psum(weighted_log, 'view'))]
    pallas_call x4, Pallas kernels: 54.8 us -> 124 us  [call(): pl.pallas_call(kernel, out_shape=jax.ShapeDtypeStruct(shape, jnp.float32)...]
  transfers between devices with their start and end apart: 12 -> 10, of which waited for: 7 -> 5; matrix products, arithmetic and copies ran while one was open for 4% -> 7% of each run, Pallas kernels for 0% -> 0%
where the time goes in v2:
time: 202 us; the launch traced here: 201 us
  Pallas kernels  124 us (61%)
  waiting for transfers between devices  27.9 us (14%)
  starting transfers between devices  27.3 us (14%)
  other arithmetic  12.7 us (6%)
  local copies, waits for them, and re-layouts  5.26 us (3%)
  between operations  4.01 us (2%)
    pallas_call x4, Pallas kernels, call(): pl.pallas_call(kernel, out_shape=jax.ShapeDtypeStruct(shape, jnp.float32)...  124 us
    ppermute x5, waiting for transfers between devices, halo(): lax.ppermute(lax.slice_in_dim(block, 0, width, axis=dim), axis, backward)  22.5 us
    ppermute x5, starting transfers between devices, halo(): lax.ppermute(lax.slice_in_dim(block, 0, width, axis=dim), axis, backward)  16.5 us
    ppermute x5, starting transfers between devices, halo(): lax.ppermute(lax.slice_in_dim(block, block.shape[dim] - width, None, axis...  10.8 us
    concatenate x1, other arithmetic, on_device(): extended = jnp.concatenate([low, observed[0], high], axis=0)  7.81 us
    ppermute x5, waiting for transfers between devices, halo(): lax.ppermute(lax.slice_in_dim(block, block.shape[dim] - width, None, axis...  5.41 us
  transfers between devices with their start and end apart: 10, of which 5 were waited for; matrix products, arithmetic and copies ran while one was open for 7% of the time, Pallas kernels for 0%

profile of v2, /device:TPU:4, one launch (start us, length us, event | category | flops | bytes accessed | tf_op | source)
XLA Modules:
  0.0 201.3 jit_solution(11173756315072635060)
XLA Ops:
  0.0 1.9 slice_bitcast_fusion
  1.9 2.8 %collective-permute-start.3 = (bf16[8,128,128]{2,1,0:T(8,128)(2,1)}, bf16[8,128,128]{2,1,0:T(8,128)(2,1)S(1)}, u32[]{:S(2)}, u32[]{:S(2)}) collective-permute-start(bf16[8,128,128]{2,1,0:T(8,128)(2,1)} %get-tuple-element.11), channel_id=1, source_target_pairs={{4,0},{8,4},{12,8},{16,12},{20,16},{24,20},{28,24},{5,1},{9,5},{13... | collective-permute-start | bytes 786440 | tf_op jit(solution)/shard_map/ppermute | solution.py:29
  4.6 1.9 collective-permute-start.2
  6.6 1.8 convert_element_type.14
  9.4 4.7 %collective-permute-start.1 = (bf16[16,128,128]{2,1,0:T(8,128)(2,1)}, bf16[16,128,128]{2,1,0:T(8,128)(2,1)S(1)}, u32[]{:S(2)}, u32[]{:S(2)}) collective-permute-start(bf16[16,128,128]{2,1,0:T(8,128)(2,1)} %get-tuple-element.13), channel_id=1, source_target_pairs={{4,0},{8,4},{12,8},{16,12},{20,16},{24,20},{28,24},{5,1},{9,5},{13... | collective-permute-start | bytes 1572872 | tf_op jit(solution)/shard_map/ppermute | solution.py:29
  14.1 1.9 collective-permute-start
  16.0 2.7 %iota_compare_fusion = (pred[48,144,144]{2,1,0:T(8,128)(4,1)}, pred[48,144,144]{2,1,0:T(8,128)(4,1)}) fusion(), kind=kLoop, calls=%fused_computation | loop fusion | flops 1990656 | bytes 1990656 | tf_op jit(solution)/shard_map/jit(_pad)/pad | solution.py:306
  23.2 7.8 %fusion.10.registered = bf16[32,128,128]{2,1,0:T(8,128)(2,1)S(1)} fusion(s32[]{:T(128)S(6)} %select_n.9, s32[]{:T(128)S(6)} %select_n.10, s32[]{:T(128)S(6)} %select_n.11, bf16[8,128,128]{2,1,0:T(8,128)(2,1)} %collective-permute-done.2, bf16[32,128,128]{2,1,0:T(8,128)(2,1)} %bitcast.23, pred[48,144,144]{2,1,0:T(8,128)(4,1)} %get-tuple-element.18, ...), kind=kLoop, calls=%fused_computation.18 | loop fusion | flops 12582912 | bytes 3672576 | tf_op jit(solution)/shard_map/concatenate | solution.py:305
  31.0 13.2 %shard_map.73.own = f32[32,128,128]{2,1,0:T(8,128)S(1)} custom-call(f32[2,3,31]{2,1,0:T(4,128)S(1)} %bitcast.15, f32[2]{0:T(128)S(1)} %bitcast.19, bf16[16,128,128]{2,1,0:T(8,128)(2,1)S(1)} %collective-permute-done.low, f32[32,128,128]{2,1,0:T(8,128)S(1)} %copy-done, bf16[16,128,128]{2,1,0:T(8,128)(2,1)S(1)} %collective-permute-done.1.high, ...), custom_call_target="tpu_custom_call" | custom-call | flops 2415919104 | bytes 6291456 | tf_op jit(solution)/shard_map/pallas_call | solution.py:277
  44.5 4.5 %collective-permute-start.5 = (bf16[16,128,128]{2,1,0:T(8,128)(2,1)S(1)}, bf16[16,128,128]{2,1,0:T(8,128)(2,1)S(1)}, u32[]{:S(2)}, u32[]{:S(2)}) collective-permute-start(bf16[16,128,128]{2,1,0:T(8,128)(2,1)S(1)} %get-tuple-element.9), channel_id=1, source_target_pairs={{4,0},{8,4},{12,8},{16,12},{20,16},{24,20},{28,24},{5,1},{9,5},{13... | collective-permute-start | bytes 1572872 | tf_op jit(solution)/shard_map/ppermute | solution.py:29
  49.0 2.1 %collective-permute-start.4 = (bf16[16,128,128]{2,1,0:T(8,128)(2,1)S(1)}, bf16[16,128,128]{2,1,0:T(8,128)(2,1)S(1)}, u32[]{:S(2)}, u32[]{:S(2)}) collective-permute-start(bf16[16,128,128]{2,1,0:T(8,128)(2,1)S(1)} %get-tuple-element.10), channel_id=1, source_target_pairs={{0,4},{4,8},{8,12},{12,16},{16,20},{20,24},{24,28},{1,5},{5,9},{9,... | collective-permute-start | bytes 1572872 | tf_op jit(solution)/shard_map/ppermute | solution.py:26
  51.2 10.0 %collective-permute-done.5.high = bf16[16,128,128]{2,1,0:T(8,128)(2,1)S(1)} collective-permute-done((bf16[16,128,128]{2,1,0:T(8,128)(2,1)S(1)}, bf16[16,128,128]{2,1,0:T(8,128)(2,1)S(1)}, u32[]{:S(2)}, u32[]{:S(2)}) %collective-permute-start.5) | collective-permute-done | bytes 524320 | tf_op jit(solution)/shard_map/ppermute | solution.py:29
  61.2 47.8 %shard_map.74.own.field = f32[32,128,128]{2,1,0:T(8,128)S(1)} custom-call(f32[2,3,31]{2,1,0:T(4,128)S(1)} %bitcast.16, f32[2]{0:T(128)S(1)} %bitcast.20, s32[4]{0:T(128)S(1)} %copy-done.2, s32[4]{0:T(128)S(1)} %copy-done.3, bf16[16,128,128]{2,1,0:T(8,128)(2,1)S(1)} %collective-permute-done.4.low, f32[32,128,128]{2,1,0:T(8,128)S(1)} %shard_map.73.own, ...), custom_call_target="tpu_custom_call" | custom-call | flops 2415919104 | bytes 6291456 | tf_op jit(solution)/shard_map/pallas_call | solution.py:277
  109.2 1.9 collective-permute-start.7
  111.2 2.4 %collective-permute-start.6 = (bf16[16,128,128]{2,1,0:T(8,128)(2,1)S(1)}, bf16[16,128,128]{2,1,0:T(8,128)(2,1)S(1)}, u32[]{:S(2)}, u32[]{:S(2)}) collective-permute-start(bf16[16,128,128]{2,1,0:T(8,128)(2,1)S(1)} %get-tuple-element.8), channel_id=1, source_target_pairs={{0,4},{4,8},{8,12},{12,16},{16,20},{20,24},{24,28},{1,5},{5,9},{9,... | collective-permute-start | bytes 1572872 | tf_op jit(solution)/shard_map/ppermute | solution.py:26
  113.6 6.8 %collective-permute-done.7.high = bf16[16,128,128]{2,1,0:T(8,128)(2,1)S(1)} collective-permute-done((bf16[16,128,128]{2,1,0:T(8,128)(2,1)S(1)}, bf16[16,128,128]{2,1,0:T(8,128)(2,1)S(1)}, u32[]{:S(2)}, u32[]{:S(2)}) %collective-permute-start.7) | collective-permute-done | bytes 524320 | tf_op jit(solution)/shard_map/ppermute | solution.py:29
  120.4 2.1 %collective-permute-done.6.low = bf16[16,128,128]{2,1,0:T(8,128)(2,1)S(1)} collective-permute-done((bf16[16,128,128]{2,1,0:T(8,128)(2,1)S(1)}, bf16[16,128,128]{2,1,0:T(8,128)(2,1)S(1)}, u32[]{:S(2)}, u32[]{:S(2)}) %collective-permute-start.6) | collective-permute-done | bytes 524320 | tf_op jit(solution)/shard_map/ppermute | solution.py:26
  122.6 13.1 %shard_map.75.own = f32[32,128,128]{2,1,0:T(8,128)S(1)} custom-call(f32[2,3,31]{2,1,0:T(4,128)S(1)} %bitcast.17, f32[2]{0:T(128)S(1)} %bitcast.21, bf16[16,128,128]{2,1,0:T(8,128)(2,1)S(1)} %collective-permute-done.6.low, f32[32,128,128]{2,1,0:T(8,128)S(1)} %shard_map.74.own.field, bf16[16,128,128]{2,1,0:T(8,128)(2,1)S(1)} %collective-permute-done.7.high, ...), custom_call_target="tpu_custom_call" | custom-call | flops 2415919104 | bytes 6291456 | tf_op jit(solution)/shard_map/pallas_call | solution.py:277
  136.0 2.6 %collective-permute-start.9 = (bf16[16,128,128]{2,1,0:T(8,128)(2,1)S(1)}, bf16[16,128,128]{2,1,0:T(8,128)(2,1)S(1)}, u32[]{:S(2)}, u32[]{:S(2)}) collective-permute-start(bf16[16,128,128]{2,1,0:T(8,128)(2,1)S(1)} %get-tuple-element.5), channel_id=1, source_target_pairs={{4,0},{8,4},{12,8},{16,12},{20,16},{24,20},{28,24},{5,1},{9,5},{13... | collective-permute-start | bytes 1572872 | tf_op jit(solution)/shard_map/ppermute | solution.py:29
  138.6 2.5 %collective-permute-start.8 = (bf16[16,128,128]{2,1,0:T(8,128)(2,1)S(1)}, bf16[16,128,128]{2,1,0:T(8,128)(2,1)S(1)}, u32[]{:S(2)}, u32[]{:S(2)}) collective-permute-start(bf16[16,128,128]{2,1,0:T(8,128)(2,1)S(1)} %get-tuple-element.6), channel_id=1, source_target_pairs={{0,4},{4,8},{8,12},{12,16},{16,20},{20,24},{24,28},{1,5},{5,9},{9,... | collective-permute-start | bytes 1572872 | tf_op jit(solution)/shard_map/ppermute | solution.py:26
  141.1 5.6 %collective-permute-done.9.high = bf16[16,128,128]{2,1,0:T(8,128)(2,1)S(1)} collective-permute-done((bf16[16,128,128]{2,1,0:T(8,128)(2,1)S(1)}, bf16[16,128,128]{2,1,0:T(8,128)(2,1)S(1)}, u32[]{:S(2)}, u32[]{:S(2)}) %collective-permute-start.9) | collective-permute-done | bytes 524320 | tf_op jit(solution)/shard_map/ppermute | solution.py:29
  146.7 3.3 %collective-permute-done.8.low = bf16[16,128,128]{2,1,0:T(8,128)(2,1)S(1)} collective-permute-done((bf16[16,128,128]{2,1,0:T(8,128)(2,1)S(1)}, bf16[16,128,128]{2,1,0:T(8,128)(2,1)S(1)}, u32[]{:S(2)}, u32[]{:S(2)}) %collective-permute-start.8) | collective-permute-done | bytes 524320 | tf_op jit(solution)/shard_map/ppermute | solution.py:26
  150.0 50.0 %shard_map.76 = f32[32,128,128]{2,1,0:T(8,128)S(1)} custom-call(f32[2,3,31]{2,1,0:T(4,128)S(1)} %bitcast.18, f32[2]{0:T(128)S(1)} %bitcast.22, s32[4]{0:T(128)S(1)} %copy-done.2, s32[4]{0:T(128)S(1)} %copy-done.3, bf16[16,128,128]{2,1,0:T(8,128)(2,1)S(1)} %collective-permute-done.8.low, f32[32,128,128]{2,1,0:T(8,128)S(1)} %shard_map.75.own, ...), custom_call_target="tpu_custom_call" | custom-call | flops 2415919104 | bytes 6291456 | tf_op jit(solution)/shard_map/pallas_call | solution.py:277
  200.0 1.3 copy.12
  (26 shorter events, 2.5 us)
Async XLA Ops:
  1.9 21.3 %collective-permute-start.3 = (bf16[8,128,128]{2,1,0:T(8,128)(2,1)}, bf16[8,128,128]{2,1,0:T(8,128)(2,1)S(1)}, u32[]{:S(2)}, u32[]{:S(2)}) collective-permute-start(bf16[8,128,128]{2,1,0:T(8,128)(2,1)} %get-tuple-element.11), channel_id=1, source_target_pairs={{4,0},{8,4},{12,8},{16,12},{20,16},{24,20},{28,24},{5,1},{9,5},{13... | collective-permute-start | bytes 786440 | tf_op jit(solution)/shard_map/ppermute | solution.py:29
  4.6 18.5 %collective-permute-start.2 = (bf16[8,128,128]{2,1,0:T(8,128)(2,1)}, bf16[8,128,128]{2,1,0:T(8,128)(2,1)}, u32[]{:S(2)}, u32[]{:S(2)}) collective-permute-start(bf16[8,128,128]{2,1,0:T(8,128)(2,1)} %get-tuple-element.12), channel_id=1, source_target_pairs={{0,4},{4,8},{8,12},{12,16},{16,20},{20,24},{24,28},{1,5},{5,9},{9,... | collective-permute-start | bytes 786440 | tf_op jit(solution)/shard_map/ppermute | solution.py:26
  9.4 9.3 %copy-start.4 = (s32[1,3]{1,0:T(1,128)S(1)}, s32[1,3]{1,0:T(1,128)}, u32[]{:S(2)}) copy-start(s32[1,3]{1,0:T(1,128)} %param.11) | copy-start | bytes 40
  9.4 13.7 %copy-start.5 = (f32[1,2,3,31]{3,1,2,0:T(2,128)S(1)}, f32[1,2,3,31]{3,1,2,0:T(2,128)}, u32[]{:S(2)}) copy-start(f32[1,2,3,31]{3,1,2,0:T(2,128)} %param.9) | copy-start | bytes 2236
  9.4 21.6 %collective-permute-start.1 = (bf16[16,128,128]{2,1,0:T(8,128)(2,1)}, bf16[16,128,128]{2,1,0:T(8,128)(2,1)S(1)}, u32[]{:S(2)}, u32[]{:S(2)}) collective-permute-start(bf16[16,128,128]{2,1,0:T(8,128)(2,1)} %get-tuple-element.13), channel_id=1, source_target_pairs={{4,0},{8,4},{12,8},{16,12},{20,16},{24,20},{28,24},{5,1},{9,5},{13... | collective-permute-start | bytes 1572872 | tf_op jit(solution)/shard_map/ppermute | solution.py:29
  14.1 16.9 %collective-permute-start = (bf16[16,128,128]{2,1,0:T(8,128)(2,1)}, bf16[16,128,128]{2,1,0:T(8,128)(2,1)S(1)}, u32[]{:S(2)}, u32[]{:S(2)}) collective-permute-start(bf16[16,128,128]{2,1,0:T(8,128)(2,1)} %get-tuple-element.14), channel_id=1, source_target_pairs={{0,4},{4,8},{8,12},{12,16},{16,20},{20,24},{24,28},{1,5},{5,9},{9,... | collective-permute-start | bytes 1572872 | tf_op jit(solution)/shard_map/ppermute | solution.py:26
  18.7 12.3 %copy-start = (f32[32,128,128]{2,1,0:T(8,128)S(1)}, f32[32,128,128]{2,1,0:T(8,128)}, u32[]{:S(2)}) copy-start(f32[32,128,128]{2,1,0:T(8,128)} %field.1) | copy-start | bytes 6291460
  18.7 12.3 %copy-start.1 = (f32[1,2]{1,0:T(1,128)S(1)}, f32[1,2]{1,0:T(1,128)}, u32[]{:S(2)}) copy-start(f32[1,2]{1,0:T(1,128)} %param.10) | copy-start | bytes 28
  44.2 17.0 %copy-start.2 = (s32[4]{0:T(128)S(1)}, s32[4]{0:T(128)}, u32[]{:S(2)}) copy-start(s32[4]{0:T(128)} %first.3) | copy-start | bytes 52
  44.2 17.0 %copy-start.3 = (s32[4]{0:T(128)S(1)}, s32[4]{0:T(128)}, u32[]{:S(2)}) copy-start(s32[4]{0:T(128)} %count.3) | copy-start | bytes 52
  44.5 16.7 %collective-permute-start.5 = (bf16[16,128,128]{2,1,0:T(8,128)(2,1)S(1)}, bf16[16,128,128]{2,1,0:T(8,128)(2,1)S(1)}, u32[]{:S(2)}, u32[]{:S(2)}) collective-permute-start(bf16[16,128,128]{2,1,0:T(8,128)(2,1)S(1)} %get-tuple-element.9), channel_id=1, source_target_pairs={{4,0},{8,4},{12,8},{16,12},{20,16},{24,20},{28,24},{5,1},{9,5},{13... | collective-permute-start | bytes 1572872 | tf_op jit(solution)/shard_map/ppermute | solution.py:29
  49.0 12.1 %collective-permute-start.4 = (bf16[16,128,128]{2,1,0:T(8,128)(2,1)S(1)}, bf16[16,128,128]{2,1,0:T(8,128)(2,1)S(1)}, u32[]{:S(2)}, u32[]{:S(2)}) collective-permute-start(bf16[16,128,128]{2,1,0:T(8,128)(2,1)S(1)} %get-tuple-element.10), channel_id=1, source_target_pairs={{0,4},{4,8},{8,12},{12,16},{16,20},{20,24},{24,28},{1,5},{5,9},{9,... | collective-permute-start | bytes 1572872 | tf_op jit(solution)/shard_map/ppermute | solution.py:26
  109.2 11.2 %collective-permute-start.7 = (bf16[16,128,128]{2,1,0:T(8,128)(2,1)S(1)}, bf16[16,128,128]{2,1,0:T(8,128)(2,1)S(1)}, u32[]{:S(2)}, u32[]{:S(2)}) collective-permute-start(bf16[16,128,128]{2,1,0:T(8,128)(2,1)S(1)} %get-tuple-element.7), channel_id=1, source_target_pairs={{4,0},{8,4},{12,8},{16,12},{20,16},{24,20},{28,24},{5,1},{9,5},{13... | collective-permute-start | bytes 1572872 | tf_op jit(solution)/shard_map/ppermute | solution.py:29
  111.2 11.4 %collective-permute-start.6 = (bf16[16,128,128]{2,1,0:T(8,128)(2,1)S(1)}, bf16[16,128,128]{2,1,0:T(8,128)(2,1)S(1)}, u32[]{:S(2)}, u32[]{:S(2)}) collective-permute-start(bf16[16,128,128]{2,1,0:T(8,128)(2,1)S(1)} %get-tuple-element.8), channel_id=1, source_target_pairs={{0,4},{4,8},{8,12},{12,16},{16,20},{20,24},{24,28},{1,5},{5,9},{9,... | collective-permute-start | bytes 1572872 | tf_op jit(solution)/shard_map/ppermute | solution.py:26
  136.0 10.7 %collective-permute-start.9 = (bf16[16,128,128]{2,1,0:T(8,128)(2,1)S(1)}, bf16[16,128,128]{2,1,0:T(8,128)(2,1)S(1)}, u32[]{:S(2)}, u32[]{:S(2)}) collective-permute-start(bf16[16,128,128]{2,1,0:T(8,128)(2,1)S(1)} %get-tuple-element.5), channel_id=1, source_target_pairs={{4,0},{8,4},{12,8},{16,12},{20,16},{24,20},{28,24},{5,1},{9,5},{13... | collective-permute-start | bytes 1572872 | tf_op jit(solution)/shard_map/ppermute | solution.py:29
  138.6 11.4 %collective-permute-start.8 = (bf16[16,128,128]{2,1,0:T(8,128)(2,1)S(1)}, bf16[16,128,128]{2,1,0:T(8,128)(2,1)S(1)}, u32[]{:S(2)}, u32[]{:S(2)}) collective-permute-start(bf16[16,128,128]{2,1,0:T(8,128)(2,1)S(1)} %get-tuple-element.6), channel_id=1, source_target_pairs={{0,4},{4,8},{8,12},{12,16},{16,20},{20,24},{24,28},{1,5},{5,9},{9,... | collective-permute-start | bytes 1572872 | tf_op jit(solution)/shard_map/ppermute | solution.py:26

commit v3 on v1

v3 whole, which is shorter than its diff:
```python
import math

import jax
import jax.numpy as jnp
from jax import lax
from jax.experimental import pallas as pl
from jax.experimental.pallas import tpu as pltpu
from jax.sharding import PartitionSpec as P

SHIFT_MAX = 8
ROUNDS = 2
HALF_TAPS = 15
HALO = 16
OFFSET = 0.1
GROUP = 16
CHUNK = 4
PIECE = 8
KNEE = 0.05
LIMIT = 24.0
UNIT = math.log(1.0 + LIMIT / KNEE) / 32767.0


def split(value):
    high = value.astype(jnp.bfloat16)
    low = (value - high.astype(jnp.float32)).astype(jnp.bfloat16)
    return high, low


def dot(a, b):
    return jnp.dot(a, b, preferred_element_type=jnp.float32)


def band(taps, rank, factor, diff, reverse):
    count = taps.shape[2]
    matrix = jnp.zeros(diff.shape, jnp.float32)
    total = jnp.float32(0.0)
    for place in range(count):
        tap = taps[rank, factor, count - 1 - place if reverse else place]
        total = total + tap
        matrix = jnp.where(diff == place, tap, matrix)
    return matrix / jnp.full(diff.shape, total, jnp.float32)


def iota(shape, dim):
    return lax.broadcasted_iota(jnp.int32, shape, dim)


def blur_tables(taps, weight, planes, width, rows, cols, reverse, mat_x, mat_y, mat_z):
    half = HALF_TAPS
    weight_sum = weight[0] + weight[1]
    shape = (planes, 4 * width)
    part = iota(shape, 1) // width
    diff = iota(shape, 1) % width - iota(shape, 0) - (HALO - half)
    for rank in range(2):
        scale = jnp.full(shape, weight[rank], jnp.float32) / jnp.full(shape, weight_sum, jnp.float32)
        full = band(taps, rank, 0, diff, reverse) * scale
        high = full.astype(jnp.bfloat16).astype(jnp.float32)
        mixed = jnp.where(part < 2, high, jnp.where(part == 2, full - high, 0.0))
        mat_x[rank * planes : (rank + 1) * planes, :] = mixed.astype(jnp.bfloat16)
        shape_y = (rows, rows)
        high, low = split(
            band(taps, rank, 1, iota(shape_y, 1) - iota(shape_y, 0) + half, reverse)
        )
        mat_y[:rows, rank * rows : (rank + 1) * rows] = high
        mat_y[rows:, rank * rows : (rank + 1) * rows] = low
        shape_z = (cols, cols)
        high, low = split(
            band(taps, rank, 2, iota(shape_z, 0) - iota(shape_z, 1) + half, reverse)
        )
        for copy in range(2):
            mat_z[rank, copy * cols : (copy + 1) * cols, :cols] = high
            mat_z[rank, copy * cols : (copy + 1) * cols, cols:] = low


def blur_xz(window, middle, mat_x, mat_z, planes, width, rows, cols):
    def first(step, carry):
        base = step * GROUP
        parts = []
        for k in range(GROUP // 2):
            sides = []
            for side in range(2):
                y = base + 2 * k + side
                high, low = split(window[pl.ds(y, width, stride=rows), :])
                sides.append(jnp.concatenate([high, low, high], axis=0))
            both = dot(mat_x[:, : 3 * width], jnp.concatenate(sides, axis=1))
            parts.append(both[:, :cols])
            parts.append(both[:, cols:])
        for rank in range(2):
            stack = jnp.concatenate(
                [p[rank * planes : (rank + 1) * planes] for p in parts], axis=0
            )
            high, low = split(stack)
            both = dot(jnp.concatenate([high, low], axis=1), mat_z[rank])
            result = both[:, :cols] + both[:, cols:]
            for k in range(GROUP):
                middle[pl.ds(rank * planes * rows + base + k, planes, stride=rows), :] = result[
                    k * planes : (k + 1) * planes
                ]
        return carry

    lax.fori_loop(0, rows // GROUP, first, 0)


def blur_y(middle, mat_y, planes, rows, cols, start, number, finish):
    def second(step, carry):
        x = start + 2 * step
        highs, lows = [], []
        for side in range(2):
            data = [
                middle[pl.ds(pl.multiple_of((rank * planes + x + side) * rows, 8), rows), :]
                for rank in range(2)
            ]
            high, low = split(jnp.concatenate(data, axis=0))
            highs.append(high)
            lows.append(low)
        both = dot(mat_y[...], jnp.concatenate(highs, axis=1))
        result = both[:rows] + both[rows:]
        result = result + dot(mat_y[:rows, :], jnp.concatenate(lows, axis=1))
        finish(2 * step, result[:, :cols])
        finish(2 * step + 1, result[:, cols:])
        return carry

    lax.fori_loop(0, number // 2, second, 0)


def encode(value):
    size = jnp.log(1.0 + jnp.abs(value) * (1.0 / KNEE)) * (1.0 / UNIT) + 0.5
    size = jnp.minimum(size, 32767.0)
    return jnp.where(value < 0.0, -size, size).astype(jnp.int32).astype(jnp.int16)


def decode(code):
    value = code.astype(jnp.int32).astype(jnp.float32)
    size = KNEE * (jnp.exp(UNIT * jnp.abs(value)) - 1.0)
    return jnp.where(value < 0.0, -size, size)


MESH = pl.DeviceIdType.MESH


def kernel(
    taps, weight, shifts, first, count, estimate, observed, out,
    window, middle, mats_x, mats_y, mats_z, extended, registered, mine,
    edge_out, edge_in, send, recv,
    seen_send, seen_recv, edge_send, edge_recv, sum_send, sum_recv,
):
    planes, rows, cols = estimate.shape
    width = planes + 2 * HALO
    blocks = lax.axis_size("blk")
    view = lax.axis_index("view")
    block = lax.axis_index("blk")
    partner = view + 1 - 2 * lax.rem(view, 2)
    inner = (view == 1) | (view == 2)
    outer = (view == 0) | (view == 3)
    has_low = block > 0
    has_high = block < blocks - 1
    starts = [0, planes // 2, PIECE, planes // 2 + PIECE]

    barrier = pltpu.get_barrier_semaphore()
    pl.semaphore_signal(barrier, inc=1, device_id={"view": partner}, device_id_type=MESH)

    @pl.when(inner)
    def _():
        pl.semaphore_signal(barrier, inc=1, device_id={"view": 3 - view}, device_id_type=MESH)

    @pl.when(has_low)
    def _():
        pl.semaphore_signal(barrier, inc=1, device_id={"blk": block - 1}, device_id_type=MESH)

    @pl.when(has_high)
    def _():
        pl.semaphore_signal(barrier, inc=1, device_id={"blk": block + 1}, device_id_type=MESH)

    def seen_copy(side):
        low = side == 0
        here = pl.ds(0, SHIFT_MAX) if low else pl.ds(planes - SHIFT_MAX, SHIFT_MAX)
        there = pl.ds(planes + SHIFT_MAX, SHIFT_MAX) if low else pl.ds(0, SHIFT_MAX)
        return pltpu.make_async_remote_copy(
            src_ref=observed.at[0, here],
            dst_ref=extended.at[there],
            send_sem=seen_send.at[side],
            recv_sem=seen_recv.at[side],
            device_id={"blk": block - 1 if low else block + 1},
            device_id_type=MESH,
        )

    def edge_copy(turn, piece):
        low = piece % 2 == 0
        place = (piece // 2) * PIECE
        return pltpu.make_async_remote_copy(
            src_ref=edge_out.at[turn, pl.ds(starts[piece], PIECE)],
            dst_ref=edge_in.at[turn, 1 if low else 0, pl.ds(place, PIECE)],
            send_sem=edge_send.at[turn, piece],
            recv_sem=edge_recv.at[turn, piece],
            device_id={"blk": block - 1 if low else block + 1},
            device_id_type=MESH,
        )

    def start_edge(turn, piece):
        @pl.when(has_low if piece % 2 == 0 else has_high)
        def _():
            edge_copy(turn, piece).start()

    def take_edges(turn):
        for piece in range(4):
            @pl.when(has_high if piece % 2 == 0 else has_low)
            def _():
                edge_copy(turn, piece).wait_recv()

        size = HALO * rows

        def body(place, carry):
            at = pl.multiple_of(place * rows, 8)
            window[pl.ds(at, rows), :] = edge_in[turn, 0, place].astype(jnp.float32)
            at = pl.multiple_of(size + (planes + place) * rows, 8)
            window[pl.ds(at, rows), :] = edge_in[turn, 1, place].astype(jnp.float32)
            return carry

        lax.fori_loop(0, HALO, body, 0)

    def set_own(turn, x, value):
        window[pl.ds(pl.multiple_of((HALO + x) * rows, 8), rows), :] = value
        edge_out[turn, x] = value.astype(jnp.bfloat16)

    def begin(x, carry):
        set_own(0, x, estimate[x])
        return carry

    lax.fori_loop(0, planes, begin, 0)

    @pl.when(block == 0)
    def _():
        extended[:SHIFT_MAX] = jnp.zeros((SHIFT_MAX, rows, cols), jnp.bfloat16)
        for turn in range(2 * ROUNDS):
            edge_in[turn, 0] = jnp.zeros((HALO, rows, cols), jnp.bfloat16)

    @pl.when(block == blocks - 1)
    def _():
        extended[planes + SHIFT_MAX :] = jnp.zeros((SHIFT_MAX, rows, cols), jnp.bfloat16)
        for turn in range(2 * ROUNDS):
            edge_in[turn, 1] = jnp.zeros((HALO, rows, cols), jnp.bfloat16)

    pl.semaphore_wait(
        barrier,
        1 + inner.astype(jnp.int32) + has_low.astype(jnp.int32) + has_high.astype(jnp.int32),
    )
    for piece in range(4):
        start_edge(0, piece)

    @pl.when(has_low)
    def _():
        seen_copy(0).start()

    @pl.when(has_high)
    def _():
        seen_copy(1).start()

    for way in range(2):
        blur_tables(
            taps, weight, planes, width, rows, cols, way == 1,
            mats_x.at[way], mats_y.at[way], mats_z.at[way],
        )
    extended[SHIFT_MAX : planes + SHIFT_MAX] = observed[0]
    covered = jnp.float32(0.0)
    owned = jnp.float32(0.0)
    for slot in range(first.shape[0]):
        inside = (block >= first[slot]) & (block < first[slot] + count[slot])
        covered = covered + jnp.where(inside, 1.0, 0.0)
        owned = owned + jnp.where(inside & (view == slot), 1.0, 0.0)
    share = jnp.full((rows, cols), owned, jnp.float32) / jnp.full((rows, cols), covered, jnp.float32)

    def register():
        @pl.when(has_high)
        def _():
            seen_copy(0).wait_recv()

        @pl.when(has_low)
        def _():
            seen_copy(1).wait_recv()

        shape_y, shape_z = (rows, rows), (cols, cols)
        shift_y = (iota(shape_y, 1) - iota(shape_y, 0) == shifts[0, 1]).astype(jnp.float32)
        shift_z = (iota(shape_z, 0) - iota(shape_z, 1) == shifts[0, 2]).astype(jnp.float32)
        shift_y, shift_z = shift_y.astype(jnp.bfloat16), shift_z.astype(jnp.bfloat16)

        def body(step, carry):
            x = 2 * step
            at = x + SHIFT_MAX + shifts[0, 0]
            both = jnp.concatenate([extended[at], extended[at + 1]], axis=0)
            both = dot(both, shift_z).astype(jnp.bfloat16)
            both = dot(shift_y, jnp.concatenate([both[:rows], both[rows:]], axis=1))
            registered[x] = both[:, :cols] + OFFSET
            registered[x + 1] = both[:, cols:] + OFFSET
            return carry

        lax.fori_loop(0, planes // 2, body, 0)

    def sum_copy(turn, stage, chunk):
        here = pl.ds(order[chunk], CHUNK)
        return pltpu.make_async_remote_copy(
            src_ref=send.at[turn, stage, here],
            dst_ref=recv.at[turn, stage, here],
            send_sem=sum_send.at[turn, stage, chunk],
            recv_sem=sum_recv.at[turn, stage, chunk],
            device_id={"view": 3 - view if stage == 1 else partner},
            device_id_type=MESH,
        )

    order = [start + part for start in starts for part in range(0, PIECE, CHUNK)]
    chunks = len(order)

    for turn in range(ROUNDS):
        mat_x, mat_y, mat_z = mats_x.at[0], mats_y.at[0], mats_z.at[0]
        take_edges(2 * turn)
        blur_xz(window, middle, mat_x, mat_z, planes, width, rows, cols)
        if turn == 0:
            register()
        for piece in range(4):
            def ratio(place, value):
                x = starts[piece] + place
                set_own(2 * turn + 1, x, registered[x] / (value + OFFSET))

            blur_y(middle, mat_y, planes, rows, cols, starts[piece], PIECE, ratio)
            start_edge(2 * turn + 1, piece)

        mat_x, mat_y, mat_z = mats_x.at[1], mats_y.at[1], mats_z.at[1]
        take_edges(2 * turn + 1)
        blur_xz(window, middle, mat_x, mat_z, planes, width, rows, cols)

        def produce(chunk):
            def give(place, value):
                log = share * jnp.log(value)
                mine[order[chunk] + place] = log
                send[turn, 0, order[chunk] + place] = encode(log)

            blur_y(middle, mat_y, planes, rows, cols, order[chunk], CHUNK, give)

            @pl.when(outer)
            def _():
                sum_copy(turn, 0, chunk).start()

        def add_pair(chunk):
            sum_copy(turn, 0, chunk).wait_recv()

            def body(place, carry):
                x = order[chunk] + place
                send[turn, 1, x] = encode(mine[x] + decode(recv[turn, 0, x]))
                return carry

            lax.fori_loop(0, CHUNK, body, 0)
            sum_copy(turn, 1, chunk).start()

        def update(x, code):
            old = estimate[x] if turn == 0 else out[x]
            new = old * jnp.exp(decode(code))
            out[x] = new
            if turn < ROUNDS - 1:
                set_own(2 * turn + 2, x, new)

        def pass_on(chunk):
            if turn < ROUNDS - 1 and chunk % 2 == 1:
                start_edge(2 * turn + 2, chunk // 2)

        def add_across(chunk):
            sum_copy(turn, 1, chunk).wait_recv()

            def body(place, carry):
                x = order[chunk] + place
                send[turn, 2, x] = encode(decode(send[turn, 1, x]) + decode(recv[turn, 1, x]))
                return carry

            lax.fori_loop(0, CHUNK, body, 0)
            sum_copy(turn, 2, chunk).start()

            def apply(place, carry):
                x = order[chunk] + place
                update(x, send[turn, 2, x])
                return carry

            lax.fori_loop(0, CHUNK, apply, 0)
            pass_on(chunk)

        def take_total(chunk):
            sum_copy(turn, 2, chunk).wait_recv()

            def apply(place, carry):
                x = order[chunk] + place
                update(x, recv[turn, 2, x])
                return carry

            lax.fori_loop(0, CHUNK, apply, 0)
            pass_on(chunk)

        for chunk in range(chunks):
            produce(chunk)
            if chunk % 4 == 3:
                @pl.when(inner)
                def _():
                    add_pair(chunk // 4)

        @pl.when(inner)
        def _():
            for chunk in range(2, chunks):
                add_pair(chunk)
                add_across(chunk - 2)
            add_across(chunks - 2)
            add_across(chunks - 1)

        @pl.when(outer)
        def _():
            for chunk in range(chunks):
                take_total(chunk)

    @pl.when(has_low)
    def _():
        seen_copy(0).wait_send()
        for turn in range(2 * ROUNDS):
            edge_copy(turn, 0).wait_send()
            edge_copy(turn, 2).wait_send()

    @pl.when(has_high)
    def _():
        seen_copy(1).wait_send()
        for turn in range(2 * ROUNDS):
            edge_copy(turn, 1).wait_send()
            edge_copy(turn, 3).wait_send()

    for turn in range(ROUNDS):
        @pl.when(outer)
        def _():
            for chunk in range(chunks):
                sum_copy(turn, 0, chunk).wait_send()

        @pl.when(inner)
        def _():
            for chunk in range(chunks):
                sum_copy(turn, 1, chunk).wait_send()
                sum_copy(turn, 2, chunk).wait_send()


def on_device(estimate, observed, psf_taps, psf_weight, shifts, cover_first, cover_count):
    planes, rows, cols = estimate.shape
    width = planes + 2 * HALO
    smem = pl.BlockSpec(memory_space=pltpu.SMEM)
    vmem = pl.BlockSpec(memory_space=pltpu.VMEM)
    dma = pltpu.SemaphoreType.DMA
    return pl.pallas_call(
        kernel,
        out_shape=jax.ShapeDtypeStruct(estimate.shape, jnp.float32),
        in_specs=[smem] * 5 + [vmem] * 2,
        out_specs=vmem,
        scratch_shapes=[
            pltpu.VMEM(((width + 1) * rows, cols), jnp.float32),
            pltpu.VMEM(((2 * planes + 1) * rows, cols), jnp.float32),
            pltpu.VMEM((2, 2 * planes, 4 * width), jnp.bfloat16),
            pltpu.VMEM((2, 2 * rows, 2 * rows), jnp.bfloat16),
            pltpu.VMEM((2, 2, 2 * cols, 2 * cols), jnp.bfloat16),
            pltpu.VMEM((planes + 2 * SHIFT_MAX, rows, cols), jnp.bfloat16),
            pltpu.VMEM((planes, rows, cols), jnp.float32),
            pltpu.VMEM((planes, rows, cols), jnp.float32),
            pltpu.VMEM((2 * ROUNDS, planes, rows, cols), jnp.bfloat16),
            pltpu.VMEM((2 * ROUNDS, 2, HALO, rows, cols), jnp.bfloat16),
            pltpu.VMEM((ROUNDS, 3, planes, rows, cols), jnp.int16),
            pltpu.VMEM((ROUNDS, 3, planes, rows, cols), jnp.int16),
            dma((2,)),
            dma((2,)),
            dma((2 * ROUNDS, 4)),
            dma((2 * ROUNDS, 4)),
            dma((ROUNDS, 3, planes // CHUNK)),
            dma((ROUNDS, 3, planes // CHUNK)),
        ],
        compiler_params=pltpu.CompilerParams(
            vmem_limit_bytes=56 * 2**20, collective_id=0, has_side_effects=True
        ),
        cost_estimate=pl.CostEstimate(
            flops=48 * planes * rows * cols * 3 * cols,
            bytes_accessed=12 * planes * rows * cols,
            transcendentals=0,
        ),
    )(psf_taps[0], psf_weight[0], shifts, cover_first, cover_count, estimate, observed)


def solution(mesh):
    placed = (
        P("blk", None, None),
        P("view", "blk", None, None),
        P("view", None, None, None),
        P("view", None),
        P("view", None),
        P(),
        P(),
    )
    return jax.shard_map(
        on_device, mesh=mesh, in_specs=placed, out_specs=P("blk", None, None), check_vma=False
    )
```

time: 332 us -> 155 us (0.47)
  waiting for transfers between devices: 207 us -> 0 us
  Pallas kernels: 54.8 us -> 151 us
  starting transfers between devices: 27 us -> 0 us
  other arithmetic: 18.5 us -> 0 us
  between operations: 17.4 us -> 0.01 us
    psum x2 -> x0, waiting for transfers between devices: 177 us -> none  [on_device(): field = field * jnp.exp(lax.psum(weighted_log, 'view'))]
    pallas_call x4 -> x1, Pallas kernels: 54.8 us -> 151 us  [on_device(): pl.pallas_call(kernel, out_shape=jax.ShapeDtypeStruct(estimate.shape, jnp...]
    ppermute x10 -> x0, waiting for transfers between devices: 30.4 us -> none  [the longest x5 25.4 us: halo(): lax.ppermute(lax.slice_in_dim(block, 0, width, axis=dim), axis, backward)]
    ppermute x10 -> x0, starting transfers between devices: 27 us -> none  [the longest x5 16.7 us: halo(): lax.ppermute(lax.slice_in_dim(block, 0, width, axis=dim), axis, backward)]
    concatenate x1 -> x0, other arithmetic: 7.8 us -> none  [on_device(): extended = jnp.concatenate([low, observed[0], high], axis=0)]
    convert_element_type x4 -> x0, other arithmetic: 4.72 us -> none  [the longest x1 2.66 us: on_device(): field_low, field_high = halo(field.astype(jnp.bfloat16), 'blk', 0, HALO)]
  transfers between devices with their start and end apart: 12 -> 0, of which waited for: 7 -> 0; matrix products, arithmetic and copies ran while one was open for 4% -> 0% of each run, Pallas kernels for 0% -> 0%
where the time goes in v3:
time: 155 us
  Pallas kernels  151 us (97%)
  local copies, waits for them, and re-layouts  4.41 us (3%)
    pallas_call x1, Pallas kernels, on_device(): pl.pallas_call(kernel, out_shape=jax.ShapeDtypeStruct(estimate.shape, jnp...  151 us
    unnamed x2, local copies, waits for them, and re-layouts  4.41 us

profile of v3, /device:TPU:4, one launch (start us, length us, event | category | flops | bytes accessed | tf_op | source)
XLA Modules:
  0.0 155.1 jit_solution(12640979622004772526)
XLA Ops:
  0.0 1.3 copy.10
  1.3 150.7 %shard_map.73 = f32[32,128,128]{2,1,0:T(8,128)} custom-call(f32[2,3,31]{2,1,0:T(4,128)} %bitcast.4, f32[2]{0:T(128)} %bitcast.5, s32[1,3]{1,0:T(1,128)} %shifts.1, s32[4]{0:T(128)} %first.1, s32[4]{0:T(128)} %count.1, f32[32,128,128]{2,1,0:T(8,128)} %estimate.1, bf16[1,32,128,128]{3,2,1,0:T(8,128)(2,1)} %observed.1), custom_call_target="tpu_custom_call" | custom-call | flops 9663676416 | bytes 6291456 | tf_op jit(solution)/shard_map/pallas_call | solution.py:447
  152.0 3.1 %copy.12 = f32[32,128,128]{2,1,0:T(8,128)} copy(f32[32,128,128]{2,1,0:T(8,128)} %shard_map.73) | data formatting | bytes 4194304

commit v4 on v3

--- a/solution.py
+++ b/solution.py
@@ -12,9 +12,9 @@
 HALF_TAPS = 15
 HALO = 16
 OFFSET = 0.1
-GROUP = 16
-CHUNK = 4
-PIECE = 8
+GROUP = 32
+CHUNK = 2
+PIECE = 4
 KNEE = 0.05
 LIMIT = 24.0
 UNIT = math.log(1.0 + LIMIT / KNEE) / 32767.0
@@ -49,13 +49,16 @@
     half = HALF_TAPS
     weight_sum = weight[0] + weight[1]
     shape = (planes, 4 * width)
-    part = iota(shape, 1) // width
-    diff = iota(shape, 1) % width - iota(shape, 0) - (HALO - half)
+    column = iota(shape, 1)
+    middle = column - width + HALO
+    last = column - width - planes
+    source = jnp.where(column < width, column, jnp.where(last < 0, middle, last))
+    diff = source - iota(shape, 0) - (HALO - half)
     for rank in range(2):
         scale = jnp.full(shape, weight[rank], jnp.float32) / jnp.full(shape, weight_sum, jnp.float32)
         full = band(taps, rank, 0, diff, reverse) * scale
         high = full.astype(jnp.bfloat16).astype(jnp.float32)
-        mixed = jnp.where(part < 2, high, jnp.where(part == 2, full - high, 0.0))
+        mixed = jnp.where(last < 0, high, jnp.where(last < width, full - high, 0.0))
         mat_x[rank * planes : (rank + 1) * planes, :] = mixed.astype(jnp.bfloat16)
         shape_y = (rows, rows)
         high, low = split(
@@ -81,8 +84,9 @@
             for side in range(2):
                 y = base + 2 * k + side
                 high, low = split(window[pl.ds(y, width, stride=rows), :])
+                low = low[HALO : HALO + planes]
                 sides.append(jnp.concatenate([high, low, high], axis=0))
-            both = dot(mat_x[:, : 3 * width], jnp.concatenate(sides, axis=1))
+            both = dot(mat_x[:, : 2 * width + planes], jnp.concatenate(sides, axis=1))
             parts.append(both[:, :cols])
             parts.append(both[:, cols:])
         for rank in range(2):
@@ -102,12 +106,12 @@
 
 
 def blur_y(middle, mat_y, planes, rows, cols, start, number, finish):
-    def second(step, carry):
-        x = start + 2 * step
+    for step in range(number // 2):
         highs, lows = [], []
         for side in range(2):
+            x = start + 2 * step + side
             data = [
-                middle[pl.ds(pl.multiple_of((rank * planes + x + side) * rows, 8), rows), :]
+                middle[(rank * planes + x) * rows : (rank * planes + x + 1) * rows, :]
                 for rank in range(2)
             ]
             high, low = split(jnp.concatenate(data, axis=0))
@@ -118,9 +122,6 @@
         result = result + dot(mat_y[:rows, :], jnp.concatenate(lows, axis=1))
         finish(2 * step, result[:, :cols])
         finish(2 * step + 1, result[:, cols:])
-        return carry
-
-    lax.fori_loop(0, number // 2, second, 0)
 
 
 def encode(value):
@@ -154,7 +155,8 @@
     outer = (view == 0) | (view == 3)
     has_low = block > 0
     has_high = block < blocks - 1
-    starts = [0, planes // 2, PIECE, planes // 2 + PIECE]
+    starts = [side + place for place in range(0, HALO, PIECE) for side in (0, planes - HALO)]
+    pieces = len(starts)
 
     barrier = pltpu.get_barrier_semaphore()
     pl.semaphore_signal(barrier, inc=1, device_id={"view": partner}, device_id_type=MESH)
@@ -202,7 +204,7 @@
             edge_copy(turn, piece).start()
 
     def take_edges(turn):
-        for piece in range(4):
+        for piece in range(pieces):
             @pl.when(has_high if piece % 2 == 0 else has_low)
             def _():
                 edge_copy(turn, piece).wait_recv()
@@ -244,16 +246,17 @@
         barrier,
         1 + inner.astype(jnp.int32) + has_low.astype(jnp.int32) + has_high.astype(jnp.int32),
     )
-    for piece in range(4):
+
+    @pl.when(has_low)
+    def _():
+        seen_copy(0).start()
+
+    @pl.when(has_high)
+    def _():
+        seen_copy(1).start()
+
+    for piece in range(pieces):
         start_edge(0, piece)
-
-    @pl.when(has_low)
-    def _():
-        seen_copy(0).start()
-
-    @pl.when(has_high)
-    def _():
-        seen_copy(1).start()
 
     for way in range(2):
         blur_tables(
@@ -308,14 +311,15 @@
 
     order = [start + part for start in starts for part in range(0, PIECE, CHUNK)]
     chunks = len(order)
+    each = PIECE // CHUNK
 
     for turn in range(ROUNDS):
         mat_x, mat_y, mat_z = mats_x.at[0], mats_y.at[0], mats_z.at[0]
+        if turn == 0:
+            register()
         take_edges(2 * turn)
         blur_xz(window, middle, mat_x, mat_z, planes, width, rows, cols)
-        if turn == 0:
-            register()
-        for piece in range(4):
+        for piece in range(pieces):
             def ratio(place, value):
                 x = starts[piece] + place
                 set_own(2 * turn + 1, x, registered[x] / (value + OFFSET))
@@ -327,17 +331,18 @@
         take_edges(2 * turn + 1)
         blur_xz(window, middle, mat_x, mat_z, planes, width, rows, cols)
 
-        def produce(chunk):
+        def produce(piece):
             def give(place, value):
                 log = share * jnp.log(value)
-                mine[order[chunk] + place] = log
-                send[turn, 0, order[chunk] + place] = encode(log)
-
-            blur_y(middle, mat_y, planes, rows, cols, order[chunk], CHUNK, give)
+                mine[starts[piece] + place] = log
+                send[turn, 0, starts[piece] + place] = encode(log)
+
+            blur_y(middle, mat_y, planes, rows, cols, starts[piece], PIECE, give)
 
             @pl.when(outer)
             def _():
-                sum_copy(turn, 0, chunk).start()
+                for part in range(each):
+                    sum_copy(turn, 0, each * piece + part).start()
 
         def add_pair(chunk):
             sum_copy(turn, 0, chunk).wait_recv()
@@ -347,7 +352,7 @@
                 send[turn, 1, x] = encode(mine[x] + decode(recv[turn, 0, x]))
                 return carry
 
-            lax.fori_loop(0, CHUNK, body, 0)
+            lax.fori_loop(0, CHUNK, body, 0, unroll=True)
             sum_copy(turn, 1, chunk).start()
 
         def update(x, code):
@@ -358,8 +363,8 @@
                 set_own(2 * turn + 2, x, new)
 
         def pass_on(chunk):
-            if turn < ROUNDS - 1 and chunk % 2 == 1:
-                start_edge(2 * turn + 2, chunk // 2)
+            if turn < ROUNDS - 1 and chunk % each == each - 1:
+                start_edge(2 * turn + 2, chunk // each)
 
         def add_across(chunk):
             sum_copy(turn, 1, chunk).wait_recv()
@@ -369,7 +374,7 @@
                 send[turn, 2, x] = encode(decode(send[turn, 1, x]) + decode(recv[turn, 1, x]))
                 return carry
 
-            lax.fori_loop(0, CHUNK, body, 0)
+            lax.fori_loop(0, CHUNK, body, 0, unroll=True)
             sum_copy(turn, 2, chunk).start()
 
             def apply(place, carry):
@@ -377,7 +382,7 @@
                 update(x, send[turn, 2, x])
                 return carry
 
-            lax.fori_loop(0, CHUNK, apply, 0)
+            lax.fori_loop(0, CHUNK, apply, 0, unroll=True)
             pass_on(chunk)
 
         def take_total(chunk):
@@ -388,15 +393,15 @@
                 update(x, recv[turn, 2, x])
                 return carry
 
-            lax.fori_loop(0, CHUNK, apply, 0)
+            lax.fori_loop(0, CHUNK, apply, 0, unroll=True)
             pass_on(chunk)
 
-        for chunk in range(chunks):
-            produce(chunk)
-            if chunk % 4 == 3:
+        for piece in range(pieces):
+            produce(piece)
+            if piece in (pieces // 2, pieces - 1):
                 @pl.when(inner)
                 def _():
-                    add_pair(chunk // 4)
+                    add_pair(0 if piece < pieces - 1 else 1)
 
         @pl.when(inner)
         def _():
@@ -415,15 +420,15 @@
     def _():
         seen_copy(0).wait_send()
         for turn in range(2 * ROUNDS):
-            edge_copy(turn, 0).wait_send()
-            edge_copy(turn, 2).wait_send()
+            for piece in range(0, pieces, 2):
+                edge_copy(turn, piece).wait_send()
 
     @pl.when(has_high)
     def _():
         seen_copy(1).wait_send()
         for turn in range(2 * ROUNDS):
-            edge_copy(turn, 1).wait_send()
-            edge_copy(turn, 3).wait_send()
+            for piece in range(1, pieces, 2):
+                edge_copy(turn, piece).wait_send()
 
     for turn in range(ROUNDS):
         @pl.when(outer)
@@ -464,8 +469,8 @@
             pltpu.VMEM((ROUNDS, 3, planes, rows, cols), jnp.int16),
             dma((2,)),
             dma((2,)),
-            dma((2 * ROUNDS, 4)),
-            dma((2 * ROUNDS, 4)),
+            dma((2 * ROUNDS, 2 * HALO // PIECE)),
+            dma((2 * ROUNDS, 2 * HALO // PIECE)),
             dma((ROUNDS, 3, planes // CHUNK)),
             dma((ROUNDS, 3, planes // CHUNK)),
         ],

time: 155 us -> 149 us (0.961)
  Pallas kernels: 151 us -> 144 us
    pallas_call x1, Pallas kernels: 151 us -> 144 us  [on_device(): pl.pallas_call(kernel, out_shape=jax.ShapeDtypeStruct(estimate.shape, jnp...]
where the time goes in v4:
time: 149 us
  Pallas kernels  144 us (97%)
  local copies, waits for them, and re-layouts  4.41 us (3%)
    pallas_call x1, Pallas kernels, on_device(): pl.pallas_call(kernel, out_shape=jax.ShapeDtypeStruct(estimate.shape, jnp...  144 us
    unnamed x2, local copies, waits for them, and re-layouts  4.41 us

profile of v4, /device:TPU:4, one launch (start us, length us, event | category | flops | bytes accessed | tf_op | source)
XLA Modules:
  0.0 148.8 jit_solution(14334312455827215290)
XLA Ops:
  0.0 1.3 copy.10
  1.3 144.4 %shard_map.73 = f32[32,128,128]{2,1,0:T(8,128)} custom-call(f32[2,3,31]{2,1,0:T(4,128)} %bitcast.4, f32[2]{0:T(128)} %bitcast.5, s32[1,3]{1,0:T(1,128)} %shifts.1, s32[4]{0:T(128)} %first.1, s32[4]{0:T(128)} %count.1, f32[32,128,128]{2,1,0:T(8,128)} %estimate.1, bf16[1,32,128,128]{3,2,1,0:T(8,128)(2,1)} %observed.1), custom_call_target="tpu_custom_call" | custom-call | flops 9663676416 | bytes 6291456 | tf_op jit(solution)/shard_map/pallas_call | solution.py:452
  145.7 3.1 %copy.12 = f32[32,128,128]{2,1,0:T(8,128)} copy(f32[32,128,128]{2,1,0:T(8,128)} %shard_map.73) | data formatting | bytes 4194304
